TPU v7x, 32 devices: a whole 2x2x4 slice. The times are simulated.
32 devices in a mesh: tp: 4 (over z), ep: 8 (over y, x, core).
Axes of the slice: x: 2, y: 2, z: 4, core: 2. Of those that a mesh axis runs over, the one named last changes fastest.
Arguments:
- hidden_in: bfloat16 [4096, 3584], P(('ep', 'tp')), may hold values from -6 to 6
- cotangent: bfloat16 [4096, 3584], P(('ep', 'tp')), may hold values from -8 to 8
- routes: int32 [4096, 2], P(('ep', 'tp')), may hold values from 0 to 63, all different within a row; in each aligned block of 128 rows (0 to 127, 128 to 255, ...) at most 4 rows name the same one
- gate_values: float32 [4096, 2], P(('ep', 'tp')), may hold values from 0.25 to 1
- dense_gate: bfloat16 [2432, 3584], P('tp'), may hold values from -0.09375 to 0.09375
- dense_up: bfloat16 [2432, 3584], P('tp'), may hold values from -0.09375 to 0.09375
- dense_down: bfloat16 [2432, 3584], P('tp', 'ep'), may hold values from -0.125 to 0.125
- expert_gate: bfloat16 [4, 4864, 3584], P('tp', 'ep'), may hold values from -0.09375 to 0.09375
- expert_up: bfloat16 [4, 4864, 3584], P('tp', 'ep'), may hold values from -0.09375 to 0.09375
- expert_down: bfloat16 [4, 4864, 3584], P('tp', 'ep'), may hold values from -0.078125 to 0.078125
Outputs:
- grad_input: bfloat16 [4096, 3584], P(('ep', 'tp'))
- grad_dense_gate: bfloat16 [2432, 3584], P('tp', 'ep')
- grad_dense_up: bfloat16 [2432, 3584], P('tp', 'ep')
- grad_dense_down: bfloat16 [2432, 3584], P('tp', 'ep')
- grad_expert_gate: bfloat16 [4, 4864, 3584], P('tp', 'ep')
- grad_expert_up: bfloat16 [4, 4864, 3584], P('tp', 'ep')
- grad_expert_down: bfloat16 [4, 4864, 3584], P('tp', 'ep')
Inputs may be any that keep to these rules, and one draw needn't show every extreme that they name: `routes`: the two experts of a token differ. Among the tokens of one aligned block of 128 rows no expert is named more than 4 times, a bound that some block reaches; every expert is named somewhere.
All inputs are finite; a program needn't handle non-finite values.
Results may differ from a plain program's by a relative error of at most 0.012.
Values may be sent and summed in bfloat16 or wider, within the bound.
No kernel may reach another device: no remote copies, remote signals or barrier semaphores. Data moves between devices by JAX's collectives and lax.ppermute only.
A program may use at most 192 MiB of HBM per device.

v0:
```python
import jax
import jax.numpy as jnp
from jax import lax
from jax.experimental import pallas as pl
from jax.experimental.pallas import tpu as pltpu
from jax.sharding import PartitionSpec as P

CAP = 4
CONTRACT = (((1,), (1,)), ((), ()))
LEADING = (((0,), (0,)), ((), ()))
F32 = jnp.float32
BF16 = jnp.bfloat16


def swiglu_backward(gate_pre, up_pre, grad_act):
    sigmoid_gate = jax.nn.sigmoid(gate_pre)
    silu_gate = gate_pre * sigmoid_gate
    act = (silu_gate * up_pre).astype(BF16)
    silu_slope = sigmoid_gate * (1.0 + gate_pre * (1.0 - sigmoid_gate))
    grad_gate = (grad_act * up_pre * silu_slope).astype(BF16)
    grad_up = (grad_act * silu_gate).astype(BF16)
    return act, grad_gate, grad_up


def slot_tables(routes, gate_values, me, experts):
    tok_count = routes.shape[0]
    named = lax.rem(me + jnp.arange(experts, dtype=jnp.int32), experts)
    onehot = (routes.reshape(-1)[:, None] == named[None, :]).astype(jnp.int32)
    before = jnp.cumsum(onehot, axis=0) - onehot
    slot = onehot[:, :, None] * (before[:, :, None] == jnp.arange(CAP, dtype=jnp.int32)).astype(
        jnp.int32
    )
    slot = slot.reshape(tok_count, 2, experts * CAP).astype(F32)
    dispatch = jnp.sum(slot, axis=1).T.astype(BF16)
    weight = jnp.sum(slot * gate_values[:, :, None], axis=(0, 1))
    return dispatch, weight


def shift(x, axis, size, by):
    return lax.ppermute(x, axis, [(i, (i + by) % size) for i in range(size)])


def slots_to_send(hidden_in, cotangent, dispatch, weight, experts):
    width = hidden_in.shape[1]
    rows = jnp.dot(dispatch, hidden_in, preferred_element_type=F32).astype(BF16)
    cots = jnp.dot(dispatch, cotangent, preferred_element_type=F32)
    cots = (cots * weight[:, None]).astype(BF16)
    return jnp.stack(
        [rows.reshape(experts, CAP, width), cots.reshape(experts, CAP, width)], axis=1
    )


def exchange_slots(sent, me, experts):
    width = sent.shape[3]
    sent = jnp.roll(sent, me, axis=0)
    got = lax.all_to_all(sent, "tp", split_axis=0, concat_axis=0, tiled=True)
    return got.transpose(1, 0, 2, 3).reshape(2, experts * CAP, width)


def expert_layer(slot_rows, slot_cot, gate_weight, up_weight, down_weight):
    e_gate = lax.dot_general(slot_rows, gate_weight, CONTRACT, preferred_element_type=F32)
    e_up = lax.dot_general(slot_rows, up_weight, CONTRACT, preferred_element_type=F32)
    e_grad_act = lax.dot_general(slot_cot, down_weight, CONTRACT, preferred_element_type=F32)
    e_act, e_grad_gate, e_grad_up = swiglu_backward(e_gate, e_up, e_grad_act)
    g_down = lax.dot_general(e_act, slot_cot, LEADING, preferred_element_type=F32).astype(BF16)
    g_gate = lax.dot_general(e_grad_gate, slot_rows, LEADING, preferred_element_type=F32).astype(
        BF16
    )
    g_up = lax.dot_general(e_grad_up, slot_rows, LEADING, preferred_element_type=F32).astype(BF16)
    terms = jnp.dot(e_grad_gate, gate_weight, preferred_element_type=F32) + jnp.dot(
        e_grad_up, up_weight, preferred_element_type=F32
    )
    return g_gate, g_up, g_down, terms.astype(BF16)


def slots_back(own, experts):
    own = own.reshape(experts, CAP, own.shape[1])
    return lax.all_to_all(own, "tp", split_axis=0, concat_axis=0, tiled=True)


def to_tokens(back, dispatch, me, experts):
    dispatch = jnp.roll(dispatch.reshape(experts, CAP, -1), me, axis=0)
    return lax.dot_general(
        dispatch.reshape(experts * CAP, -1),
        back.reshape(experts * CAP, -1),
        LEADING,
        preferred_element_type=F32,
    )


def plain_block(rows, cot, gate, up, down):
    gate_pre = lax.dot_general(rows, gate, CONTRACT, preferred_element_type=F32)
    up_pre = lax.dot_general(rows, up, CONTRACT, preferred_element_type=F32)
    grad_act = lax.dot_general(cot, down, CONTRACT, preferred_element_type=F32)
    act, grad_gate, grad_up = swiglu_backward(gate_pre, up_pre, grad_act)
    partial = jnp.dot(grad_gate, gate, preferred_element_type=F32) + jnp.dot(
        grad_up, up, preferred_element_type=F32
    )
    return act, grad_gate, grad_up, partial.astype(BF16)


VMEM_LIMIT = 20 * 1024 * 1024
VMEM_ALL = 60 * 1024 * 1024


def unit_tiles(units):
    return [(start, min(256, units - start)) for start in range(0, units, 256)]


def layer_kernel(rows, cots, gate, up, down, down_turned, turned, partials, col, ready=None):
    units, width = gate.shape
    for t, (start, size) in enumerate(unit_tiles(units)):
        if ready is not None:
            ready(t)
        gate_pre, up_pre = [
            lax.dot_general(w[start : start + size], rows, CONTRACT, preferred_element_type=F32)
            for w in (gate, up)
        ]
        if down_turned:
            grad_act = jnp.dot(
                cots, down[:, start : start + size], preferred_element_type=F32
            ).T
        else:
            grad_act = lax.dot_general(
                down[start : start + size], cots, CONTRACT, preferred_element_type=F32
            )
        for i, value in enumerate(swiglu_backward(gate_pre, up_pre, grad_act)):
            turned[i, start : start + size] = value
    grads = [turned[1].T, turned[2].T]
    for j in range(0, width, col):
        made = (
            jnp.dot(grads[0], gate[:, j : j + col], preferred_element_type=F32)
            + jnp.dot(grads[1], up[:, j : j + col], preferred_element_type=F32)
        ).astype(BF16)
        begin = 0
        for partial in partials:
            end = begin + partial.shape[0]
            partial[:, j : j + col] = made[begin:end]
            begin = end


def dense_block(core, blocks, gate, up, down):
    tok, width = blocks[0].shape[1] * len(blocks), blocks[0].shape[2]
    units = gate.shape[0]
    half = units // 2
    tiles = unit_tiles(units)

    def kernel(core_ref, *refs):
        ins, refs = refs[: len(blocks)], refs[len(blocks) :]
        gate, up, down, own, other = refs[:5]
        partials, (gate_in, up_in, down_in, turned, sems) = refs[5:-5], refs[-5:]
        copies = [
            [
                pltpu.make_async_copy(
                    source.at[pl.ds(start, size)], target.at[pl.ds(start, size)], sems.at[w, t]
                )
                for w, (source, target) in enumerate(((gate, gate_in), (up, up_in)))
            ]
            for t, (start, size) in enumerate(tiles)
        ]
        copies[0].append(pltpu.make_async_copy(down, down_in, sems.at[2, 0]))
        for group in copies:
            for copy in group:
                copy.start()

        def ready(t):
            for copy in copies[t]:
                copy.wait()

        rows, cots = [
            ins[0][k]
            if len(ins) == 1
            else jnp.concatenate([ref[k] for ref in ins], axis=0)
            for k in range(2)
        ]
        layer_kernel(rows, cots, gate_in, up_in, down_in, True, turned, partials, 512, ready)
        mine = core_ref[0]
        own[...] = turned[:, pl.ds(pl.multiple_of(mine * half, 16), half), :]
        other[...] = turned[:, pl.ds(pl.multiple_of((1 - mine) * half, 16), half), :]

    vmem = pl.BlockSpec(memory_space=pltpu.VMEM)
    hbm = pl.BlockSpec(memory_space=pl.ANY)
    return pl.pallas_call(
        kernel,
        in_specs=[pl.BlockSpec(memory_space=pltpu.SMEM)] + [vmem] * len(blocks) + [hbm] * 3,
        out_specs=[vmem] * (2 + len(blocks)),
        out_shape=[
            jax.ShapeDtypeStruct((3, half, tok), BF16),
            jax.ShapeDtypeStruct((3, half, tok), BF16),
            *[jax.ShapeDtypeStruct(b.shape[1:], BF16) for b in blocks],
        ],
        scratch_shapes=[
            pltpu.VMEM((units, width), BF16),
            pltpu.VMEM((units, width), BF16),
            pltpu.VMEM((width, units), BF16),
            pltpu.VMEM((3, units, tok), BF16),
            pltpu.SemaphoreType.DMA((3, len(tiles))),
        ],
        compiler_params=pltpu.CompilerParams(vmem_limit_bytes=VMEM_ALL),
        cost_estimate=pl.CostEstimate(
            flops=10 * units * width * tok,
            bytes_accessed=6 * units * width + 6 * tok * (width + units),
            transcendentals=units * tok,
        ),
        name="dense_block",
    )(core.reshape(1), *blocks, gate, up, down)


def expert_block(slots, gate, up, down):
    devices, _, per_device, width = slots.shape
    tok = devices * per_device
    units = gate.shape[0]
    col = 512
    tiles = unit_tiles(units)

    def kernel(
        slots, gate, up, down, g_gate, g_up, g_down, partial, loaded, turned, made, sems, out_sems
    ):
        rows, cots = [
            jnp.concatenate([slots[i, k] for i in range(devices)], axis=0) for k in range(2)
        ]
        copies = [
            [
                pltpu.make_async_copy(
                    source.at[pl.ds(start, size)], loaded.at[w, pl.ds(start, size)], sems.at[w, t]
                )
                for w, source in enumerate((gate, up, down))
            ]
            for t, (start, size) in enumerate(tiles)
        ]
        for group in copies:
            for copy in group:
                copy.start()

        def ready(t):
            for copy in copies[t]:
                copy.wait()

        layer_kernel(
            rows, cots, *[loaded.at[w] for w in range(3)], False, turned, (partial,), 512, ready
        )
        outs = (g_down, g_gate, g_up)
        pending = [None, None]
        step = 0
        for i in range(3):
            right = cots if i == 0 else rows
            for j in range(0, width, col):
                slot = step % 2
                if pending[slot] is not None:
                    pending[slot].wait()
                made[slot] = jnp.dot(
                    turned[i], right[:, j : j + col], preferred_element_type=F32
                ).astype(BF16)
                copy = pltpu.make_async_copy(
                    made.at[slot], outs[i].at[:, pl.ds(j, col)], out_sems.at[slot]
                )
                copy.start()
                pending[slot] = copy
                step += 1
        for copy in pending:
            copy.wait()

    vmem = pl.BlockSpec(memory_space=pltpu.VMEM)
    hbm = pl.BlockSpec(memory_space=pl.ANY)
    grad = jax.ShapeDtypeStruct((units, width), BF16)
    return pl.pallas_call(
        kernel,
        in_specs=[vmem, hbm, hbm, hbm],
        out_specs=[hbm, hbm, hbm, vmem],
        out_shape=[grad, grad, grad, jax.ShapeDtypeStruct((tok, width), BF16)],
        scratch_shapes=[
            pltpu.VMEM((3, units, width), BF16),
            pltpu.VMEM((3, units, tok), BF16),
            pltpu.VMEM((2, units, col), BF16),
            pltpu.SemaphoreType.DMA((3, len(tiles))),
            pltpu.SemaphoreType.DMA((2,)),
        ],
        compiler_params=pltpu.CompilerParams(vmem_limit_bytes=VMEM_ALL),
        cost_estimate=pl.CostEstimate(flops=1, bytes_accessed=1, transcendentals=0),
        name="expert_block",
    )(slots, gate, up, down)


def final_sum(core, lows, highs):
    cut, width = lows[2].shape[1:]
    units = cut + highs[2].shape[1]
    half = width // 2

    def kernel(core_ref, *refs):
        ins, (mine, other) = refs[:-2], refs[-2:]
        own_first = core_ref[0] == 0
        for i in range(3):
            for begin, (own, near, far) in ((0, ins[:3]), (cut, ins[3:])):
                total = own[i, :, width:].astype(F32) + near[i, :, width:].astype(F32)
                total = total + far[i].astype(F32)
                left, right = total[:, :half].astype(BF16), total[:, half:].astype(BF16)
                size = total.shape[0]
                mine[i, begin : begin + size] = jnp.where(own_first, left, right)
                other[i, begin : begin + size] = jnp.where(own_first, right, left)

    vmem = pl.BlockSpec(memory_space=pltpu.VMEM)
    shape = jax.ShapeDtypeStruct((3, units, half), BF16)
    return pl.pallas_call(
        kernel,
        in_specs=[pl.BlockSpec(memory_space=pltpu.SMEM)] + [vmem] * 6,
        out_specs=[vmem, vmem],
        out_shape=[shape, shape],
        compiler_params=pltpu.CompilerParams(vmem_limit_bytes=VMEM_LIMIT),
        cost_estimate=pl.CostEstimate(
            flops=9 * units * width,
            bytes_accessed=24 * units * width,
            transcendentals=0,
        ),
        name="final_sum",
    )(core.reshape(1), *lows, *highs)


def join_halves(core, mine, other):
    _, units, width = mine.shape

    def kernel(core_ref, mine, other, *outs):
        first = core_ref[0] == 0
        for i in range(3):
            a, b = mine[i], other[i]
            joined = jnp.concatenate([jnp.where(first, a, b), jnp.where(first, b, a)], axis=0)
            outs[i][...] = joined.T

    vmem = pl.BlockSpec(memory_space=pltpu.VMEM)
    grads = pl.pallas_call(
        kernel,
        in_specs=[pl.BlockSpec(memory_space=pltpu.SMEM), vmem, vmem],
        out_specs=[vmem] * 3,
        out_shape=[jax.ShapeDtypeStruct((width, 2 * units), BF16)] * 3,
        compiler_params=pltpu.CompilerParams(vmem_limit_bytes=VMEM_ALL),
        cost_estimate=pl.CostEstimate(
            flops=0, bytes_accessed=24 * units * width, transcendentals=0
        ),
        name="join_halves",
    )(core.reshape(1), mine, other)
    return [grad.T for grad in grads]


def weight_terms(tiles, acts, blocks, width, begin, end):
    units = acts[0].shape[1]
    tokens = sum(b.shape[1] for b in blocks)
    size = end - begin

    def kernel(tile_ref, *refs):
        a, b, out = refs[: len(acts)], refs[len(acts) : -1], refs[-1]
        rows = jnp.concatenate([ref[0] for ref in b], axis=0)
        cots = jnp.concatenate([ref[1] for ref in b], axis=0)
        for i in range(3):
            left = jnp.concatenate([ref[i, begin:end] for ref in a], axis=1)
            out[i] = jnp.dot(
                left, cots if i == 0 else rows, preferred_element_type=F32
            ).astype(BF16)

    def whole(shape):
        return pl.BlockSpec(shape, lambda j, tile_ref: (0, 0, 0))

    def columns(block):
        return pl.BlockSpec((*block.shape[:2], width), lambda j, tile_ref: (0, 0, tile_ref[j]))

    return pl.pallas_call(
        kernel,
        grid_spec=pltpu.PrefetchScalarGridSpec(
            num_scalar_prefetch=1,
            grid=(2,),
            in_specs=[whole(a.shape) for a in acts] + [columns(b) for b in blocks],
            out_specs=pl.BlockSpec((3, size, width), lambda j, tile_ref: (0, 0, j)),
        ),
        out_shape=jax.ShapeDtypeStruct((3, size, 2 * width), BF16),
        compiler_params=pltpu.CompilerParams(vmem_limit_bytes=VMEM_ALL),
        cost_estimate=pl.CostEstimate(
            flops=12 * size * tokens * width,
            bytes_accessed=2 * (tokens * (4 * width + 3 * units) + 6 * size * width),
            transcendentals=0,
        ),
        name="weight_terms",
    )(tiles, *acts, *blocks)


def routed_rows(hidden_in, cotangent, routes, gate_values, experts):
    tok, width = hidden_in.shape
    count = experts * 2 * CAP

    def kernel(rows, cots, routes, gates, out):
        line = lax.broadcasted_iota(jnp.int32, (count, tok), 0)
        expert, slot = line // (2 * CAP), lax.rem(line, CAP)
        first, second = routes[0:1] == expert, routes[1:2] == expert
        named = jnp.where(first | second, 1.0, 0.0)
        earlier = lax.broadcasted_iota(jnp.int32, (tok, tok), 0) < lax.broadcasted_iota(
            jnp.int32, (tok, tok), 1
        )
        before = jnp.dot(
            named.astype(BF16),
            jnp.where(earlier, 1.0, 0.0).astype(BF16),
            preferred_element_type=F32,
        )
        taken = jnp.where(before == slot.astype(F32), named, 0.0)
        weight = jnp.where(first, gates[0:1], 0.0) + jnp.where(second, gates[1:2], 0.0)
        weight = jnp.sum(taken * weight, axis=1, keepdims=True)
        taken = taken.astype(BF16)
        kept = lax.broadcasted_iota(jnp.int32, (count, 1), 0)
        is_cot = lax.rem(kept, 2 * CAP) >= CAP
        for j in range(0, width, 512):
            columns = slice(j, j + 512)
            row_part = jnp.dot(taken, rows[:, columns], preferred_element_type=F32)
            cot_part = jnp.dot(taken, cots[:, columns], preferred_element_type=F32) * weight
            out[:, columns] = jnp.where(is_cot, cot_part, row_part).astype(BF16)

    vmem = pl.BlockSpec(memory_space=pltpu.VMEM)
    return pl.pallas_call(
        kernel,
        in_specs=[vmem] * 4,
        out_specs=vmem,
        out_shape=jax.ShapeDtypeStruct((count, width), BF16),
        compiler_params=pltpu.CompilerParams(vmem_limit_bytes=VMEM_LIMIT),
        cost_estimate=pl.CostEstimate(
            flops=4 * count * tok * width, bytes_accessed=4 * tok * width, transcendentals=0
        ),
        name="routed_rows",
    )(hidden_in, cotangent, routes.T, gate_values.T)


def together(*values):
    return lax.optimization_barrier(values)


def line_body(
    hidden_in,
    cotangent,
    routes,
    gate_values,
    dense_gate,
    dense_up,
    dense_down,
    expert_gate,
    expert_up,
    expert_down,
):
    experts = lax.axis_size("tp")
    me = lax.axis_index("tp")
    ep = lax.axis_index("ep")
    core, chip = lax.rem(ep, 2), lax.div(ep, 2)
    half = dense_gate.shape[0] // 2
    columns = dense_down.shape[1]
    down = lax.all_gather(dense_down.T, "ep", axis=0, tiled=True)

    def pairs(value):
        return lax.ppermute(value, "tp", [(0, 1), (1, 0), (2, 3), (3, 2)])

    def mirror(value):
        return lax.ppermute(value, "tp", [(0, 3), (1, 2), (2, 1), (3, 0)])

    def across(value, apart):
        return lax.ppermute(value, "ep", [(i, i ^ apart) for i in range(8)])

    def add(a, b):
        return (a.astype(F32) + b.astype(F32)).astype(BF16)

    def dense(blocks):
        mine, other, *partials = dense_block(core, blocks, dense_gate, dense_up, down)
        tokens = [*blocks, *(across(b, 1) for b in blocks)]
        return ([mine, across(other, 1)], tokens), partials

    own = jnp.stack([hidden_in, cotangent])
    mirrored, paired = mirror(own), pairs(own)
    sent = routed_rows(hidden_in, cotangent, routes, gate_values, experts)
    got = lax.all_to_all(sent, "tp", split_axis=0, concat_axis=0, tiled=True)
    got = got.reshape(experts, 2, CAP, -1).transpose(1, 0, 2, 3).reshape(2, experts * CAP, -1)
    dispatch, _ = slot_tables(routes, gate_values, me, experts)
    x_chip, y_chip, xy_chip = [jnp.bitwise_xor(chip, k) for k in (1, 2, 3)]
    chip_tiles = [
        jnp.stack(t)
        for t in ((xy_chip, x_chip), (xy_chip, y_chip), (y_chip, chip), (x_chip, chip))
    ]
    both0, (partial0,) = dense([own])
    got, partial0, both0, dispatch, chip_tiles = together(
        got, partial0, both0, dispatch, chip_tiles
    )

    mirrored, paired, got = together(mirrored, paired, got)
    last = pairs(mirrored)
    slots = lax.all_gather(got, "ep", axis=0, tiled=False)
    both12, (paired_partial, mirrored_partial) = dense([paired, mirrored])
    slots, both12, paired_partial, mirrored_partial = together(
        slots, both12, paired_partial, mirrored_partial
    )
    g_gate, g_up, g_down, slot_terms = expert_block(
        slots, expert_gate[0], expert_up[0], expert_down[0]
    )

    last, both12, slot_terms = together(last, both12, slot_terms)
    routed = lax.psum_scatter(slot_terms, "ep", scatter_dimension=0, tiled=True)
    both3, (partial3,) = dense([last])
    from_last = pairs(partial3)

    acts, tokens = (a + b + c for a, b, c in zip(both0, both12, both3))
    cut, width = -(-half // 32) * 16, 2 * columns
    low_sent = weight_terms(chip_tiles[0], acts, tokens, width, 0, cut)
    high_sent = weight_terms(chip_tiles[1], acts, tokens, width, cut, half)
    high_sent, chip_tiles, from_last = together(high_sent, chip_tiles, from_last)
    low_kept = weight_terms(chip_tiles[2], acts, tokens, width, 0, cut)
    high_kept = weight_terms(chip_tiles[3], acts, tokens, width, cut, half)
    low_near, high_near = across(low_sent, 2), across(high_sent, 4)
    from_pair = pairs(paired_partial)
    low_kept, high_kept, from_pair, routed = together(low_kept, high_kept, from_pair, routed)
    back = slots_back(routed, experts)
    from_last, back = together(from_last, back)
    from_mirror = mirror(add(mirrored_partial, from_last))
    low_near, high_near, low_kept, high_kept, back = together(
        low_near, high_near, low_kept, high_kept, back
    )
    low_far = across(add(low_kept[:, :, :width], low_near[:, :, :width]), 4)
    high_far = across(add(high_kept[:, :, :width], high_near[:, :, :width]), 2)
    low_far, high_far, from_mirror = together(low_far, high_far, from_mirror)
    routed_input = to_tokens(back, dispatch, me, experts)
    mine, other = final_sum(
        core, (low_kept, low_near, low_far), (high_kept, high_near, high_far)
    )
    grads = join_halves(core, mine, across(other, 1))
    grad_input = (
        partial0.astype(F32)
        + from_pair.astype(F32)
        + from_mirror.astype(F32)
        + routed_input
    ).astype(BF16)
    return (grad_input, grads[1], grads[2], grads[0], g_gate[None], g_up[None], g_down[None])


def general_body(
    hidden_in,
    cotangent,
    routes,
    gate_values,
    dense_gate,
    dense_up,
    dense_down,
    expert_gate,
    expert_up,
    expert_down,
):
    experts = lax.axis_size("tp")
    me = lax.axis_index("tp")
    dispatch, weight = slot_tables(routes, gate_values, me, experts)
    sent = slots_to_send(hidden_in, cotangent, dispatch, weight, experts)
    got = exchange_slots(sent, me, experts)
    slots = lax.all_gather(got, "ep", axis=0, tiled=False)
    slot_rows, slot_cot = slots[:, 0].reshape(-1, hidden_in.shape[1]), slots[:, 1].reshape(
        -1, hidden_in.shape[1]
    )
    rows = lax.all_gather(hidden_in, "tp", axis=0, tiled=True)
    cots = lax.all_gather(cotangent, "tp", axis=0, tiled=True)
    down = lax.all_gather(dense_down, "ep", axis=1, tiled=True)
    act, grad_gate, grad_up, partial = plain_block(rows, cots, dense_gate, dense_up, down)
    dense_input = lax.psum_scatter(partial, "tp", scatter_dimension=0, tiled=True)
    grads = [
        lax.psum_scatter(
            lax.dot_general(a, b, LEADING, preferred_element_type=F32).astype(BF16),
            "ep",
            scatter_dimension=1,
            tiled=True,
        )
        for a, b in ((act, cots), (grad_gate, rows), (grad_up, rows))
    ]
    g_gate, g_up, g_down, slot_terms = expert_layer(
        slot_rows, slot_cot, expert_gate[0], expert_up[0], expert_down[0]
    )
    routed = lax.psum_scatter(slot_terms, "ep", scatter_dimension=0, tiled=True)
    routed_input = to_tokens(slots_back(routed, experts), dispatch, me, experts)
    grad_input = (dense_input.astype(F32) + routed_input).astype(BF16)
    return (grad_input, grads[1], grads[2], grads[0], g_gate[None], g_up[None], g_down[None])


def solution(mesh):
    placed = (
        P(("ep", "tp"), None),
        P(("ep", "tp"), None),
        P(("ep", "tp"), None),
        P(("ep", "tp"), None),
        P("tp", None),
        P("tp", None),
        P("tp", "ep"),
        P("tp", "ep", None),
        P("tp", "ep", None),
        P("tp", "ep", None),
    )
    in_line = mesh.shape["tp"] == 4 and mesh.shape["ep"] == 8
    return jax.shard_map(
        line_body if in_line else general_body,
        mesh=mesh,
        in_specs=placed,
        out_specs=(
            P(("ep", "tp"), None),
            P("tp", "ep"),
            P("tp", "ep"),
            P("tp", "ep"),
            P("tp", "ep", None),
            P("tp", "ep", None),
            P("tp", "ep", None),
        ),
        check_vma=False,
    )
```

profile of v0, /device:TPU:9, one launch (start us, length us, event | category | flops | bytes accessed | tf_op | source)
XLA Modules:
  0.0 278.1 jit_solution(6013830921144861841)
XLA Ops:
  7.2 0.7 all-gather.4.cloned.1.call-update
  7.9 1.8 pad_maximum_fusion.refs_0_.refs_6_
  9.7 0.7 collective-permute-start.1
  10.4 1.3 collective-permute-start.2
  11.8 2.2 collective-permute-start.3
  14.0 1.2 routed_rows.1
  15.2 3.4 %all-to-all-start = ((bf16[4,8,3584]{2,1,0:T(8,128)(2,1)}), bf16[4,8,3584]{2,1,0:T(8,128)(2,1)S(1)}, u32[]{:S(2)}, u32[]{:S(2)}) async-start(bf16[4,8,3584]{2,1,0:T(8,128)(2,1)} %bitcast.2), calls=%async_computation | async-start | bytes 458752 | tf_op jit(solution)/shard_map/all_to_all | solution.py:470
  18.7 0.1 eq.52
  18.9 0.1 eq.56
  19.1 1.2 reduce-window.6
  20.8 0.1 copy.34
  20.9 0.3 eq.60
  21.3 0.3 eq.61
  21.8 0.3 mul.10
  22.2 0.3 mul.11
  22.6 0.7 pad_add_fusion
  23.3 26.6 %all-gather.4.cloned.1.call-done.refs_3_.refs_4_ = bf16[3584,608]{1,0:T(8,128)(2,1)} async-done(((bf16[448,608]{1,0:T(8,128)(2,1)}), bf16[3584,608]{1,0:T(8,128)(2,1)}) %all-gather.4.cloned.1.call-update) | async-done | bytes 4358160 | tf_op jit(solution)/shard_map/all_gather | solution.py:448
  49.9 11.9 %dense_block.3 = (bf16[3,304,128]{2,1,0:T(8,128)(2,1)}, bf16[3,304,128]{2,1,0:T(8,128)(2,1)}, bf16[128,3584]{1,0:T(8,128)(2,1)}) custom-call(s32[1]{0:T(128)} %bitcast.4.core_ref, bf16[2,128,3584]{2,1,0:T(8,128)(2,1)} %copy-done.7, bf16[608,3584]{1,0:T(8,128)(2,1)} %refs_1_.3, bf16[608,3584]{1,0:T(8,128)(2,1)} %refs_2_.5, ...), custom_call_target="tpu_custom_call" | custom-call | flops 2789212160 | bytes 16293888 | tf_op jit(solution)/shard_map/dense_block/pallas_call | solution.py:183
  61.8 0.3 collective-permute-start
  62.1 0.6 pad_add_fusion.2
  62.7 0.8 fusion.1
  63.5 32.6 %all-to-all-done = bf16[4,8,3584]{2,1,0:T(8,128)(2,1)S(1)} async-done(((bf16[4,8,3584]{2,1,0:T(8,128)(2,1)}), bf16[4,8,3584]{2,1,0:T(8,128)(2,1)S(1)}, u32[]{:S(2)}, u32[]{:S(2)}) %all-to-all-start) | async-done | bytes 229408 | tf_op jit(solution)/shard_map/all_to_all | solution.py:470
  96.3 0.7 reshape.104
  97.1 0.2 reduce-scatter.2.cloned.1.call-start
  97.3 0.8 collective-permute-start.6
  98.3 1.4 collective-permute-start.4
  99.6 16.1 %dense_block.4 = (bf16[3,304,256]{2,1,0:T(8,128)(2,1)}, bf16[3,304,256]{2,1,0:T(8,128)(2,1)}, bf16[128,3584]{1,0:T(8,128)(2,1)}, bf16[128,3584]{1,0:T(8,128)(2,1)}) custom-call(s32[1]{0:T(128)} %bitcast.4.core_ref, bf16[2,128,3584]{2,1,0:T(8,128)(2,1)} %collective-permute-done.3.refs_0_.refs_8_, ...), custom_call_target="tpu_custom_call" | custom-call | flops 5578424320 | bytes 19513344 | tf_op jit(solution)/shard_map/dense_block/pallas_call | solution.py:183
  115.8 0.8 collective-permute-start.5
  116.5 1.7 collective-permute-done.5.refs_3_
  118.2 7.6 %all-gather.6.cloned.1.call-done = bf16[16,16,3584]{2,1,0:T(8,128)(2,1)} async-done(((bf16[2,16,3584]{2,1,0:T(8,128)(2,1)}), bf16[16,16,3584]{2,1,0:T(8,128)(2,1)}) %all-gather.6.cloned.1.call-update) | async-done | bytes 1835024 | tf_op jit(solution)/shard_map/all_gather | solution.py:485
  125.8 24.7 %expert_block.1 = (bf16[608,3584]{1,0:T(8,128)(2,1)}, bf16[608,3584]{1,0:T(8,128)(2,1)}, bf16[608,3584]{1,0:T(8,128)(2,1)}, bf16[128,3584]{1,0:T(8,128)(2,1)}) custom-call(bf16[8,2,16,3584]{3,2,1,0:T(8,128)(2,1)} %bitcast.51, bf16[608,3584]{1,0:T(8,128)(2,1)} %bitcast.48, bf16[608,3584]{1,0:T(8,128)(2,1)} %bitcast.49, bf16[608,3584]{1,0:T(8,128)(2,1)} %bitcast.50), custom_call_target="tpu_custom_call" | custom-call | flops 1 | bytes 1 | tf_op jit(solution)/shard_map/expert_block/pallas_call | solution.py:266
  150.5 0.3 collective-permute-start.9
  150.9 0.9 copy-done.8
  151.8 11.8 %dense_block.5 = (bf16[3,304,128]{2,1,0:T(8,128)(2,1)}, bf16[3,304,128]{2,1,0:T(8,128)(2,1)}, bf16[128,3584]{1,0:T(8,128)(2,1)}) custom-call(s32[1]{0:T(128)} %bitcast.4.core_ref, bf16[2,128,3584]{2,1,0:T(8,128)(2,1)} %copy-done.8, bf16[608,3584]{1,0:T(8,128)(2,1)} %refs_1_.3, bf16[608,3584]{1,0:T(8,128)(2,1)} %refs_2_.5, ...), custom_call_target="tpu_custom_call" | custom-call | flops 2789212160 | bytes 16293888 | tf_op jit(solution)/shard_map/dense_block/pallas_call | solution.py:183
  163.6 0.4 collective-permute-start.10
  164.0 0.6 collective-permute-start.8
  164.5 1.1 collective-permute-start.11
  165.7 0.2 collective-permute-done.8.refs_5_
  165.9 0.7 copy-done.11
  166.6 7.2 %weight_terms.7 = bf16[3,160,1792]{2,1,0:T(8,128)(2,1)} custom-call(s32[2]{0:T(128)} %get-tuple-element.109.tile_ref, bf16[3,304,128]{2,1,0:T(8,128)(2,1)} %get-tuple-element.80.refs_0_, bf16[3,304,128]{2,1,0:T(8,128)(2,1)} %copy-done.10, bf16[3,304,256]{2,1,0:T(8,128)(2,1)} %get-tuple-element.98.refs_2_, bf16[3,304,256]{2,1,0:T(8,128)(2,1)} %copy-done.9, ...), custom_call_target="tpu_custom_call" | custom-call | flops 1761607680 | bytes 10928128 | tf_op jit(solution)/shard_map/weight_terms/pallas_call | solution.py:364
  173.8 1.2 collective-permute-start.12
  174.9 7.0 %weight_terms.4 = bf16[3,144,1792]{2,1,0:T(8,128)(2,1)} custom-call(s32[2]{0:T(128)} %get-tuple-element.79.tile_ref, bf16[3,304,128]{2,1,0:T(8,128)(2,1)} %get-tuple-element.80.refs_0_, bf16[3,304,128]{2,1,0:T(8,128)(2,1)} %copy-done.10, bf16[3,304,256]{2,1,0:T(8,128)(2,1)} %get-tuple-element.98.refs_2_, bf16[3,304,256]{2,1,0:T(8,128)(2,1)} %copy-done.9, ...), custom_call_target="tpu_custom_call" | custom-call | flops 1585446912 | bytes 10756096 | tf_op jit(solution)/shard_map/weight_terms/pallas_call | solution.py:364
  182.0 3.7 %collective-permute-done.10 = bf16[128,3584]{1,0:T(8,128)(2,1)S(1)} collective-permute-done((bf16[128,3584]{1,0:T(8,128)(2,1)}, bf16[128,3584]{1,0:T(8,128)(2,1)S(1)}, u32[]{:S(2)}, u32[]{:S(2)}) %collective-permute-start.10) | collective-permute-done | bytes 917536 | tf_op jit(solution)/shard_map/ppermute | solution.py:451
  185.7 1.1 collective-permute-start.13
  186.7 7.0 %weight_terms.6.refs_3_ = bf16[3,144,1792]{2,1,0:T(8,128)(2,1)} custom-call(s32[2]{0:T(128)} %get-tuple-element.114.tile_ref, bf16[3,304,128]{2,1,0:T(8,128)(2,1)} %get-tuple-element.80.refs_0_, bf16[3,304,128]{2,1,0:T(8,128)(2,1)} %copy-done.10, bf16[3,304,256]{2,1,0:T(8,128)(2,1)} %get-tuple-element.98.refs_2_, bf16[3,304,256]{2,1,0:T(8,128)(2,1)} %copy-done.9, ...), custom_call_target="tpu_custom_call" | custom-call | flops 1585446912 | bytes 10756096 | tf_op jit(solution)/shard_map/weight_terms/pallas_call | solution.py:364
  193.7 7.2 %weight_terms.5.refs_0_ = bf16[3,160,1792]{2,1,0:T(8,128)(2,1)} custom-call(s32[2]{0:T(128)} %get-tuple-element.113.tile_ref, bf16[3,304,128]{2,1,0:T(8,128)(2,1)} %get-tuple-element.80.refs_0_, bf16[3,304,128]{2,1,0:T(8,128)(2,1)} %copy-done.10, bf16[3,304,256]{2,1,0:T(8,128)(2,1)} %get-tuple-element.98.refs_2_, bf16[3,304,256]{2,1,0:T(8,128)(2,1)} %copy-done.9, ...), custom_call_target="tpu_custom_call" | custom-call | flops 1761607680 | bytes 10928128 | tf_op jit(solution)/shard_map/weight_terms/pallas_call | solution.py:364
  201.0 4.4 %collective-permute-done.11 = bf16[128,3584]{1,0:T(8,128)(2,1)} collective-permute-done((bf16[128,3584]{1,0:T(8,128)(2,1)}, bf16[128,3584]{1,0:T(8,128)(2,1)}, u32[]{:S(2)}, u32[]{:S(2)}) %collective-permute-start.11) | collective-permute-done | bytes 917536 | tf_op jit(solution)/shard_map/ppermute | solution.py:451
  205.3 0.9 reshape.107
  206.3 8.7 %all_to_all.14 = bf16[4,4,3584]{2,1,0:T(4,128)(2,1)} all-to-all(bf16[4,4,3584]{2,1,0:T(4,128)(2,1)S(1)} %reshape.107), channel_id=1, replica_groups=mesh['tp'=4,'ep'=8] {'tp'}, dimensions={0} | all-to-all | bytes 229376 | tf_op jit(solution)/shard_map/all_to_all | solution.py:78
  214.9 1.7 add_convert_fusion.1
  216.6 0.3 collective-permute-start.16
  217.0 2.8 collective-permute-done.13.refs_4_
  219.7 0.2 add_convert_fusion.2
  219.9 1.1 collective-permute-start.14
  221.0 1.3 add_convert_fusion.3
  222.3 0.5 collective-permute-start.15
  222.9 34.5 %collective-permute-done.16 = bf16[128,3584]{1,0:T(8,128)(2,1)S(1)} collective-permute-done((bf16[128,3584]{1,0:T(8,128)(2,1)S(1)}, bf16[128,3584]{1,0:T(8,128)(2,1)S(1)}, u32[]{:S(2)}, u32[]{:S(2)}) %collective-permute-start.16) | collective-permute-done | bytes 917536 | tf_op jit(solution)/shard_map/ppermute | solution.py:454
  257.3 0.9 copy-done.15
  258.3 3.3 %final_sum.1 = (bf16[3,304,448]{2,1,0:T(8,128)(2,1)S(1)}, bf16[3,304,448]{2,1,0:T(8,128)(2,1)}) custom-call(s32[1]{0:T(128)} %bitcast.4.core_ref, bf16[3,160,1792]{2,1,0:T(8,128)(2,1)S(1)} %copy-done, bf16[3,160,1792]{2,1,0:T(8,128)(2,1)S(1)} %collective-permute-done.12.refs_1_, bf16[3,160,896]{2,1,0:T(8,128)(2,1)S(1)} %collective-permute-done.14.refs_2_, ...), custom_call_target="tpu_custom_call" | custom-call | flops 2451456 | bytes 6537216 | tf_op jit(solution)/shard_map/final_sum/pallas_call | solution.py:303
  261.6 0.9 copy-done.4
  262.6 1.8 collective-permute-start.17
  264.4 3.3 %add_convert_fusion = bf16[128,3584]{1,0:T(8,128)(2,1)} fusion(bf16[128,3584]{1,0:T(8,128)(2,1)} %copy-done.15, bf16[128,3584]{1,0:T(8,128)(2,1)} %collective-permute-done.11, bf16[128,3584]{1,0:T(8,128)(2,1)} %get-tuple-element.78, bf16[4,4,3584]{2,1,0:T(4,128)(2,1)} %all_to_all.14, s32[]{:T(128)S(6)} %select_n.14, bf16[4,4,128]{2,1,0:T(4,128)(2,1)S(1)} %bitcast.55), kind=kOutput, calls=%fused_computation.2 | convolution fusion | flops 17899520 | bytes 3788804 | tf_op jit(solution)/shard_map/dot_general | solution.py:83
  267.8 0.9 copy-done.12
  268.7 2.9 %join_halves.1 = (bf16[448,608]{1,0:T(8,128)(2,1)}, bf16[448,608]{1,0:T(8,128)(2,1)}, bf16[448,608]{1,0:T(8,128)(2,1)}) custom-call(s32[1]{0:T(128)} %bitcast.4.core_ref, bf16[3,304,448]{2,1,0:T(8,128)(2,1)} %copy-done.4, bf16[3,304,448]{2,1,0:T(8,128)(2,1)} %copy-done.12), custom_call_target="tpu_custom_call" | custom-call | bytes 3268608 | tf_op jit(solution)/shard_map/join_halves/pallas_call | solution.py:329
  (62 shorter events, 1.4 us)
Async XLA Ops:
  7.2 42.7 %all-gather.4.cloned.1.call-start = ((), (), s32[]{:S(2)}) async-start(), calls=%async_computation.3 | async-start | bytes 5160960 | tf_op jit(solution)/shard_map/all_gather | solution.py:448
  7.9 6.1 %copy-start.2 = (bf16[128,3584]{1,0:T(8,128)(2,1)S(1)}, bf16[128,3584]{1,0:T(8,128)(2,1)}, u32[]{:S(2)}) copy-start(bf16[128,3584]{1,0:T(8,128)(2,1)} %cots.1) | copy-start | bytes 2752516
  7.9 6.0 %copy-start.3 = (bf16[128,3584]{1,0:T(8,128)(2,1)S(1)}, bf16[128,3584]{1,0:T(8,128)(2,1)}, u32[]{:S(2)}) copy-start(bf16[128,3584]{1,0:T(8,128)(2,1)} %rows.1) | copy-start | bytes 2752516
  7.9 6.0 %copy-start.5 = (s32[128,2]{0,1:T(2,128)S(1)}, s32[128,2]{0,1:T(2,128)}, u32[]{:S(2)}) copy-start(s32[128,2]{0,1:T(2,128)} %param.12) | copy-start | bytes 3076
  7.9 6.0 %copy-start.6 = (f32[128,2]{0,1:T(2,128)S(1)}, f32[128,2]{0,1:T(2,128)}, u32[]{:S(2)}) copy-start(f32[128,2]{0,1:T(2,128)} %param.13) | copy-start | bytes 3076
  9.7 11.9 %copy-start.7 = (bf16[2,128,3584]{2,1,0:T(8,128)(2,1)}, bf16[2,128,3584]{2,1,0:T(8,128)(2,1)S(1)}, u32[]{:S(2)}) copy-start(bf16[2,128,3584]{2,1,0:T(8,128)(2,1)S(1)} %pad_maximum_fusion.refs_0_.refs_6_) | copy-start | bytes 5505028
  9.7 87.4 %collective-permute-start.1 = (bf16[2,128,3584]{2,1,0:T(8,128)(2,1)S(1)}, bf16[2,128,3584]{2,1,0:T(8,128)(2,1)}, u32[]{:S(2)}, u32[]{:S(2)}) collective-permute-start(bf16[2,128,3584]{2,1,0:T(8,128)(2,1)S(1)} %pad_maximum_fusion.refs_0_.refs_6_), channel_id=1, source_target_pairs={{0,1},{1,0},{2,3},{3,2},{4,5},{5,4},{6,7},{7,6},{8,9},{9,8},{10,11... | collective-permute-start | bytes 5505032 | tf_op jit(solution)/shard_map/ppermute | solution.py:457
  10.4 86.6 %collective-permute-start.2 = (bf16[2,128,3584]{2,1,0:T(8,128)(2,1)S(1)}, bf16[2,128,3584]{2,1,0:T(8,128)(2,1)}, u32[]{:S(2)}, u32[]{:S(2)}) collective-permute-start(bf16[2,128,3584]{2,1,0:T(8,128)(2,1)S(1)} %pad_maximum_fusion.refs_0_.refs_6_), channel_id=1, source_target_pairs={{0,24},{8,16},{16,8},{24,0},{1,25},{9,17},{17,9},{25,1},{2,26},{10... | collective-permute-start | bytes 5505032 | tf_op jit(solution)/shard_map/ppermute | solution.py:454
  11.8 85.3 %collective-permute-start.3 = (bf16[2,128,3584]{2,1,0:T(8,128)(2,1)S(1)}, bf16[2,128,3584]{2,1,0:T(8,128)(2,1)}, u32[]{:S(2)}, u32[]{:S(2)}) collective-permute-start(bf16[2,128,3584]{2,1,0:T(8,128)(2,1)S(1)} %pad_maximum_fusion.refs_0_.refs_6_), channel_id=1, source_target_pairs={{0,8},{8,0},{16,24},{24,16},{1,9},{9,1},{17,25},{25,17},{2,10},{10... | collective-permute-start | bytes 5505032 | tf_op jit(solution)/shard_map/ppermute | solution.py:451
  15.2 81.0 %all-to-all-start = ((bf16[4,8,3584]{2,1,0:T(8,128)(2,1)}), bf16[4,8,3584]{2,1,0:T(8,128)(2,1)S(1)}, u32[]{:S(2)}, u32[]{:S(2)}) async-start(bf16[4,8,3584]{2,1,0:T(8,128)(2,1)} %bitcast.2), calls=%async_computation | async-start | bytes 458752 | tf_op jit(solution)/shard_map/all_to_all | solution.py:470
  18.6 107.2 %all-gather.6.cloned.1.call-start = ((), (), s32[]{:S(2)}) async-start(), calls=%async_computation.5 | async-start | bytes 2064384 | tf_op jit(solution)/shard_map/all_gather | solution.py:485
  61.8 35.3 %collective-permute-start = (bf16[3,304,128]{2,1,0:T(8,128)(2,1)}, bf16[3,304,128]{2,1,0:T(8,128)(2,1)S(1)}, u32[]{:S(2)}, u32[]{:S(2)}) collective-permute-start(bf16[3,304,128]{2,1,0:T(8,128)(2,1)} %get-tuple-element.77), channel_id=1, source_target_pairs={{0,1},{1,0},{2,3},{3,2},{4,5},{5,4},{6,7},{7,6},{8,9},{9,8},{10,11... | collective-permute-start | bytes 700424 | tf_op jit(solution)/shard_map/ppermute | solution.py:457
  97.1 18.7 %copy-start.10 = (bf16[3,304,128]{2,1,0:T(8,128)(2,1)}, bf16[3,304,128]{2,1,0:T(8,128)(2,1)S(1)}, u32[]{:S(2)}) copy-start(bf16[3,304,128]{2,1,0:T(8,128)(2,1)S(1)} %collective-permute-done.refs_1_) | copy-start | bytes 700420
  97.1 108.2 %reduce-scatter.2.cloned.1.call-start = ((), (), s32[]{:S(2)}) async-start(), calls=%async_computation.4 | async-start | bytes 1032192 | tf_op jit(solution)/shard_map/reduce_scatter | solution.py:495
  97.3 20.9 %collective-permute-start.6 = (bf16[2,128,3584]{2,1,0:T(8,128)(2,1)}, bf16[2,128,3584]{2,1,0:T(8,128)(2,1)}, u32[]{:S(2)}, u32[]{:S(2)}) collective-permute-start(bf16[2,128,3584]{2,1,0:T(8,128)(2,1)} %collective-permute-done.3.refs_0_.refs_8_), channel_id=1, source_target_pairs={{0,1},{1,0},{2,3},{3,2},{4,5},{5,4},{6,7},{7,6},{8,9},{9,8},{10,11... | collective-permute-start | bytes 5505032 | tf_op jit(solution)/shard_map/ppermute | solution.py:457
  98.2 20.0 %collective-permute-start.7 = (bf16[2,128,3584]{2,1,0:T(8,128)(2,1)}, bf16[2,128,3584]{2,1,0:T(8,128)(2,1)}, u32[]{:S(2)}, u32[]{:S(2)}) collective-permute-start(bf16[2,128,3584]{2,1,0:T(8,128)(2,1)} %collective-permute-done.2.refs_1_.refs_9_), channel_id=1, source_target_pairs={{0,1},{1,0},{2,3},{3,2},{4,5},{5,4},{6,7},{7,6},{8,9},{9,8},{10,11... | collective-permute-start | bytes 5505032 | tf_op jit(solution)/shard_map/ppermute | solution.py:457
  98.3 52.3 %collective-permute-start.4 = (bf16[2,128,3584]{2,1,0:T(8,128)(2,1)}, bf16[2,128,3584]{2,1,0:T(8,128)(2,1)S(1)}, u32[]{:S(2)}, u32[]{:S(2)}) collective-permute-start(bf16[2,128,3584]{2,1,0:T(8,128)(2,1)} %collective-permute-done.2.refs_1_.refs_9_), channel_id=1, source_target_pairs={{0,8},{8,0},{16,24},{24,16},{1,9},{9,1},{17,25},{25,17},{2,10},{10... | collective-permute-start | bytes 5505032 | tf_op jit(solution)/shard_map/ppermute | solution.py:451
  115.8 2.4 collective-permute-start.5
  118.2 32.3 %copy-start.9 = (bf16[3,304,256]{2,1,0:T(8,128)(2,1)}, bf16[3,304,256]{2,1,0:T(8,128)(2,1)S(1)}, u32[]{:S(2)}) copy-start(bf16[3,304,256]{2,1,0:T(8,128)(2,1)S(1)} %collective-permute-done.5.refs_3_) | copy-start | bytes 1400836
  150.5 1.2 copy-start.8
  150.5 15.3 %collective-permute-start.9 = (bf16[2,128,3584]{2,1,0:T(8,128)(2,1)S(1)}, bf16[2,128,3584]{2,1,0:T(8,128)(2,1)}, u32[]{:S(2)}, u32[]{:S(2)}) collective-permute-start(bf16[2,128,3584]{2,1,0:T(8,128)(2,1)S(1)} %collective-permute-done.4.refs_0_.refs_12_), channel_id=1, source_target_pairs={{0,1},{1,0},{2,3},{3,2},{4,5},{5,4},{6,7},{7,6},{8,9},{9,8},{10,11... | collective-permute-start | bytes 5505032 | tf_op jit(solution)/shard_map/ppermute | solution.py:457
  163.6 22.1 %collective-permute-start.10 = (bf16[128,3584]{1,0:T(8,128)(2,1)}, bf16[128,3584]{1,0:T(8,128)(2,1)S(1)}, u32[]{:S(2)}, u32[]{:S(2)}) collective-permute-start(bf16[128,3584]{1,0:T(8,128)(2,1)} %get-tuple-element.112), channel_id=1, source_target_pairs={{0,8},{8,0},{16,24},{24,16},{1,9},{9,1},{17,25},{25,17},{2,10},{10... | collective-permute-start | bytes 2752520 | tf_op jit(solution)/shard_map/ppermute | solution.py:451
  164.0 1.9 collective-permute-start.8
  164.5 40.8 %collective-permute-start.11 = (bf16[128,3584]{1,0:T(8,128)(2,1)}, bf16[128,3584]{1,0:T(8,128)(2,1)}, u32[]{:S(2)}, u32[]{:S(2)}) collective-permute-start(bf16[128,3584]{1,0:T(8,128)(2,1)} %get-tuple-element.115), channel_id=1, source_target_pairs={{0,8},{8,0},{16,24},{24,16},{1,9},{9,1},{17,25},{25,17},{2,10},{10... | collective-permute-start | bytes 2752520 | tf_op jit(solution)/shard_map/ppermute | solution.py:451
  165.9 0.7 copy-start.11
  173.8 45.9 %collective-permute-start.12 = (bf16[3,160,1792]{2,1,0:T(8,128)(2,1)}, bf16[3,160,1792]{2,1,0:T(8,128)(2,1)S(1)}, u32[]{:S(2)}, u32[]{:S(2)}) collective-permute-start(bf16[3,160,1792]{2,1,0:T(8,128)(2,1)} %weight_terms.7), channel_id=1, source_target_pairs={{0,2},{1,3},{2,0},{3,1},{4,6},{5,7},{6,4},{7,5},{8,10},{9,11},{10,... | collective-permute-start | bytes 5160968 | tf_op jit(solution)/shard_map/ppermute | solution.py:457
  185.7 8.0 %copy-start.13 = (bf16[128,3584]{1,0:T(8,128)(2,1)}, bf16[128,3584]{1,0:T(8,128)(2,1)S(1)}, u32[]{:S(2)}) copy-start(bf16[128,3584]{1,0:T(8,128)(2,1)S(1)} %collective-permute-done.10) | copy-start | bytes 2752516
  185.7 34.0 %collective-permute-start.13 = (bf16[3,144,1792]{2,1,0:T(8,128)(2,1)}, bf16[3,144,1792]{2,1,0:T(8,128)(2,1)}, u32[]{:S(2)}, u32[]{:S(2)}) collective-permute-start(bf16[3,144,1792]{2,1,0:T(8,128)(2,1)} %weight_terms.4), channel_id=1, source_target_pairs={{0,4},{1,5},{2,6},{3,7},{4,0},{5,1},{6,2},{7,3},{8,12},{9,13},{10,... | collective-permute-start | bytes 4644872 | tf_op jit(solution)/shard_map/ppermute | solution.py:457
  200.9 18.8 %copy-start = (bf16[3,160,1792]{2,1,0:T(8,128)(2,1)S(1)}, bf16[3,160,1792]{2,1,0:T(8,128)(2,1)}, u32[]{:S(2)}) copy-start(bf16[3,160,1792]{2,1,0:T(8,128)(2,1)} %weight_terms.5.refs_0_) | copy-start | bytes 5160964
  216.6 4.4 %copy-start.1 = (bf16[3,144,1792]{2,1,0:T(8,128)(2,1)S(1)}, bf16[3,144,1792]{2,1,0:T(8,128)(2,1)}, u32[]{:S(2)}) copy-start(bf16[3,144,1792]{2,1,0:T(8,128)(2,1)} %weight_terms.6.refs_3_) | copy-start | bytes 4644868
  216.6 40.7 %collective-permute-start.16 = (bf16[128,3584]{1,0:T(8,128)(2,1)S(1)}, bf16[128,3584]{1,0:T(8,128)(2,1)S(1)}, u32[]{:S(2)}, u32[]{:S(2)}) collective-permute-start(bf16[128,3584]{1,0:T(8,128)(2,1)S(1)} %add_convert_fusion.1), channel_id=1, source_target_pairs={{0,24},{8,16},{16,8},{24,0},{1,25},{9,17},{17,9},{25,1},{2,26},{10... | collective-permute-start | bytes 2752520 | tf_op jit(solution)/shard_map/ppermute | solution.py:454
  219.9 38.3 %collective-permute-start.14 = (bf16[3,160,896]{2,1,0:T(8,128)(2,1)S(1)}, bf16[3,160,896]{2,1,0:T(8,128)(2,1)S(1)}, u32[]{:S(2)}, u32[]{:S(2)}) collective-permute-start(bf16[3,160,896]{2,1,0:T(8,128)(2,1)S(1)} %add_convert_fusion.2), channel_id=1, source_target_pairs={{0,4},{1,5},{2,6},{3,7},{4,0},{5,1},{6,2},{7,3},{8,12},{9,13},{10,... | collective-permute-start | bytes 2580488 | tf_op jit(solution)/shard_map/ppermute | solution.py:457
  222.3 42.0 %copy-start.14 = (bf16[128,16]{1,0:T(8,128)(2,1)S(1)}, bf16[128,16]{1,0:T(8,128)(2,1)}, u32[]{:S(2)}) copy-start(bf16[128,16]{1,0:T(8,128)(2,1)} %fusion.1) | copy-start | bytes 12292
  222.3 35.0 %collective-permute-start.15 = (bf16[3,144,896]{2,1,0:T(8,128)(2,1)S(1)}, bf16[3,144,896]{2,1,0:T(8,128)(2,1)S(1)}, u32[]{:S(2)}, u32[]{:S(2)}) collective-permute-start(bf16[3,144,896]{2,1,0:T(8,128)(2,1)S(1)} %add_convert_fusion.3), channel_id=1, source_target_pairs={{0,2},{1,3},{2,0},{3,1},{4,6},{5,7},{6,4},{7,5},{8,10},{9,11},{10,... | collective-permute-start | bytes 2322440 | tf_op jit(solution)/shard_map/ppermute | solution.py:457
  257.3 0.9 copy-start.15
  261.6 0.9 copy-start.4
  262.6 5.2 %collective-permute-start.17 = (bf16[3,304,448]{2,1,0:T(8,128)(2,1)}, bf16[3,304,448]{2,1,0:T(8,128)(2,1)S(1)}, u32[]{:S(2)}, u32[]{:S(2)}) collective-permute-start(bf16[3,304,448]{2,1,0:T(8,128)(2,1)} %get-tuple-element.136), channel_id=1, source_target_pairs={{0,1},{1,0},{2,3},{3,2},{4,5},{5,4},{6,7},{7,6},{8,9},{9,8},{10,11... | collective-permute-start | bytes 2451464 | tf_op jit(solution)/shard_map/ppermute | solution.py:457
  267.7 0.9 copy-start.12
Sparse Core Ops, SparseCore 0:
  9.9 39.9 all-gather.3
  97.2 28.5 all-gather.5
  151.0 36.3 reduce-scatter.1
where the time goes:
time: 279 us; the launch traced here: 278 us
  waiting for transfers between devices  115 us (41%)
  Pallas kernels  100 us (36%)
  starting transfers between devices  19.6 us (7%)
  between operations  14 us (5%)
  blocking collectives  8.68 us (3%)
  local copies, waits for them, and re-layouts  8.64 us (3%)
  other arithmetic  8.56 us (3%)
  matrix products  3.35 us (1%)
    pallas_call x3, Pallas kernels, dense_block(): pl.pallas_call(kernel, in_specs=[pl.BlockSpec(memory_space=pltpu.SMEM)] +...  39.9 us
    ppermute x2, waiting for transfers between devices, mirror(): return lax.ppermute(value, 'tp', [(0, 3), (1, 2), (2, 1), (3, 0)])  34.5 us
    all_to_all x1, waiting for transfers between devices, line_body(): got = lax.all_to_all(sent, 'tp', split_axis=0, concat_axis=0, tiled=True)  32.6 us
    pallas_call x4, Pallas kernels, weight_terms(): pl.pallas_call(kernel, grid_spec=pltpu.PrefetchScalarGridSpec(num_scalar_...  28.5 us
    all_gather x1, waiting for transfers between devices, line_body(): down = lax.all_gather(dense_down.T, 'ep', axis=0, tiled=True)  26.6 us
    pallas_call x1, Pallas kernels, expert_block(): pl.pallas_call(kernel, in_specs=[vmem, hbm, hbm, hbm], out_specs=[hbm, hb...  24.7 us
    ppermute x12, starting transfers between devices, across(): return lax.ppermute(value, 'ep', [(i, i ^ apart) for i in range(8)])  9.24 us
    all_to_all x1, blocking collectives, slots_back(): return lax.all_to_all(own, 'tp', split_axis=0, concat_axis=0, tiled=True)  8.68 us
  transfers between devices with their start and end apart: 22, of which 9 were waited for; matrix products, arithmetic and copies ran while one was open for 6% of the time, Pallas kernels for 34%

commit v1 on v0

--- a/solution.py
+++ b/solution.py
@@ -504,18 +504,16 @@
     low_kept = weight_terms(chip_tiles[2], acts, tokens, width, 0, cut)
     high_kept = weight_terms(chip_tiles[3], acts, tokens, width, cut, half)
     low_near, high_near = across(low_sent, 2), across(high_sent, 4)
+    from_mirror = mirror(add(mirrored_partial, from_last))
+    low_kept, high_kept, routed = together(low_kept, high_kept, routed)
+    low_near, high_near, low_kept, high_kept, paired_partial, routed = together(
+        low_near, high_near, low_kept, high_kept, paired_partial, routed
+    )
     from_pair = pairs(paired_partial)
-    low_kept, high_kept, from_pair, routed = together(low_kept, high_kept, from_pair, routed)
-    back = slots_back(routed, experts)
-    from_last, back = together(from_last, back)
-    from_mirror = mirror(add(mirrored_partial, from_last))
-    low_near, high_near, low_kept, high_kept, back = together(
-        low_near, high_near, low_kept, high_kept, back
-    )
     low_far = across(add(low_kept[:, :, :width], low_near[:, :, :width]), 4)
     high_far = across(add(high_kept[:, :, :width], high_near[:, :, :width]), 2)
-    low_far, high_far, from_mirror = together(low_far, high_far, from_mirror)
-    routed_input = to_tokens(back, dispatch, me, experts)
+    from_mirror, routed = together(from_mirror, routed)
+    routed_input = to_tokens(slots_back(routed, experts), dispatch, me, experts)
     mine, other = final_sum(
         core, (low_kept, low_near, low_far), (high_kept, high_near, high_far)
     )

time: 279 us -> 277 us (level)
  the two profiles are of different devices: /device:TPU:9 before, /device:TPU:0 now
where the time goes in v1:
time: 277 us; the launch traced here: 276 us
  waiting for transfers between devices  111 us (40%)
  Pallas kernels  100 us (36%)
  starting transfers between devices  25.7 us (9%)
  other arithmetic  15.8 us (6%)
  between operations  14.1 us (5%)
  local copies, waits for them, and re-layouts  8.7 us (3%)
    pallas_call x3, Pallas kernels, dense_block(): pl.pallas_call(kernel, in_specs=[pl.BlockSpec(memory_space=pltpu.SMEM)] +...  39.8 us
    all_to_all x1, waiting for transfers between devices, line_body(): got = lax.all_to_all(sent, 'tp', split_axis=0, concat_axis=0, tiled=True)  35.4 us
    pallas_call x4, Pallas kernels, weight_terms(): pl.pallas_call(kernel, grid_spec=pltpu.PrefetchScalarGridSpec(num_scalar_...  29 us
    all_gather x1, waiting for transfers between devices, line_body(): down = lax.all_gather(dense_down.T, 'ep', axis=0, tiled=True)  26.3 us
    pallas_call x1, Pallas kernels, expert_block(): pl.pallas_call(kernel, in_specs=[vmem, hbm, hbm, hbm], out_specs=[hbm, hb...  24.7 us
    reduce_scatter x1, waiting for transfers between devices, line_body(): routed = lax.psum_scatter(slot_terms, 'ep', scatter_dimension=0, tiled=True)  18.5 us
    all_to_all x1, waiting for transfers between devices, slots_back(): return lax.all_to_all(own, 'tp', split_axis=0, concat_axis=0, tiled=True)  15.9 us
    all_gather x1, waiting for transfers between devices, line_body(): slots = lax.all_gather(got, 'ep', axis=0, tiled=False)  8.12 us
  transfers between devices with their start and end apart: 23, of which 8 were waited for; matrix products, arithmetic and copies ran while one was open for 7% of the time, Pallas kernels for 35%

profile of v1, /device:TPU:0, one launch (start us, length us, event | category | flops | bytes accessed | tf_op | source)
XLA Modules:
  0.0 276.4 jit_solution(16716851104566960679)
XLA Ops:
  7.2 0.7 all-gather.4.cloned.1.call-update
  7.9 1.8 pad_maximum_fusion.refs_0_.refs_6_
  9.7 0.5 collective-permute-start.1
  10.2 2.7 collective-permute-start.3
  12.9 2.5 collective-permute-start.2
  15.4 1.2 routed_rows.1
  16.6 3.4 %all-to-all-start = ((bf16[4,8,3584]{2,1,0:T(8,128)(2,1)}), bf16[4,8,3584]{2,1,0:T(8,128)(2,1)S(1)}, u32[]{:S(2)}, u32[]{:S(2)}) async-start(bf16[4,8,3584]{2,1,0:T(8,128)(2,1)} %bitcast.2), calls=%async_computation | async-start | bytes 458752 | tf_op jit(solution)/shard_map/all_to_all | solution.py:470
  20.0 0.1 copy.30
  20.1 0.1 eq.56
  20.3 0.1 eq.52
  20.6 1.2 reduce-window.6
  21.9 0.1 copy.31
  22.2 0.1 copy.35
  22.5 0.1 copy.34
  22.6 0.3 eq.60
  23.0 0.3 eq.61
  23.3 0.3 mul.10
  23.7 0.3 mul.11
  24.0 0.7 pad_add_fusion
  24.7 26.3 %all-gather.4.cloned.1.call-done.refs_3_.refs_4_ = bf16[3584,608]{1,0:T(8,128)(2,1)} async-done(((bf16[448,608]{1,0:T(8,128)(2,1)}), bf16[3584,608]{1,0:T(8,128)(2,1)}) %all-gather.4.cloned.1.call-update) | async-done | bytes 4358160 | tf_op jit(solution)/shard_map/all_gather | solution.py:448
  51.0 11.9 %dense_block.3 = (bf16[3,304,128]{2,1,0:T(8,128)(2,1)}, bf16[3,304,128]{2,1,0:T(8,128)(2,1)}, bf16[128,3584]{1,0:T(8,128)(2,1)}) custom-call(s32[1]{0:T(128)} %bitcast.4.core_ref, bf16[2,128,3584]{2,1,0:T(8,128)(2,1)} %copy-done.9, bf16[608,3584]{1,0:T(8,128)(2,1)} %refs_1_.3, bf16[608,3584]{1,0:T(8,128)(2,1)} %refs_2_.5, ...), custom_call_target="tpu_custom_call" | custom-call | flops 2789212160 | bytes 16293888 | tf_op jit(solution)/shard_map/dense_block/pallas_call | solution.py:183
  62.9 0.3 collective-permute-start
  63.2 0.6 pad_add_fusion.2
  63.8 0.8 fusion.1
  64.7 35.4 %all-to-all-done = bf16[4,8,3584]{2,1,0:T(8,128)(2,1)S(1)} async-done(((bf16[4,8,3584]{2,1,0:T(8,128)(2,1)}), bf16[4,8,3584]{2,1,0:T(8,128)(2,1)S(1)}, u32[]{:S(2)}, u32[]{:S(2)}) %all-to-all-start) | async-done | bytes 229408 | tf_op jit(solution)/shard_map/all_to_all | solution.py:470
  100.2 0.7 reshape.104
  101.0 0.2 reduce-scatter.2.cloned.1.call-start
  101.3 0.5 collective-permute-start.7
  101.8 16.0 %dense_block.4 = (bf16[3,304,256]{2,1,0:T(8,128)(2,1)}, bf16[3,304,256]{2,1,0:T(8,128)(2,1)}, bf16[128,3584]{1,0:T(8,128)(2,1)}, bf16[128,3584]{1,0:T(8,128)(2,1)}) custom-call(s32[1]{0:T(128)} %bitcast.4.core_ref, bf16[2,128,3584]{2,1,0:T(8,128)(2,1)} %collective-permute-done.3.refs_0_.refs_8_, ...), custom_call_target="tpu_custom_call" | custom-call | flops 5578424320 | bytes 19513344 | tf_op jit(solution)/shard_map/dense_block/pallas_call | solution.py:183
  117.9 0.2 collective-permute-start.5
  118.0 2.1 collective-permute-done.5.refs_3_
  120.1 8.1 %all-gather.6.cloned.1.call-done = bf16[16,16,3584]{2,1,0:T(8,128)(2,1)} async-done(((bf16[2,16,3584]{2,1,0:T(8,128)(2,1)}), bf16[16,16,3584]{2,1,0:T(8,128)(2,1)}) %all-gather.6.cloned.1.call-update) | async-done | bytes 1835024 | tf_op jit(solution)/shard_map/all_gather | solution.py:485
  128.2 24.7 %expert_block.1 = (bf16[608,3584]{1,0:T(8,128)(2,1)}, bf16[608,3584]{1,0:T(8,128)(2,1)}, bf16[608,3584]{1,0:T(8,128)(2,1)}, bf16[128,3584]{1,0:T(8,128)(2,1)}) custom-call(bf16[8,2,16,3584]{3,2,1,0:T(8,128)(2,1)} %bitcast.49, bf16[608,3584]{1,0:T(8,128)(2,1)} %bitcast.46, bf16[608,3584]{1,0:T(8,128)(2,1)} %bitcast.47, bf16[608,3584]{1,0:T(8,128)(2,1)} %bitcast.48), custom_call_target="tpu_custom_call" | custom-call | flops 1 | bytes 1 | tf_op jit(solution)/shard_map/expert_block/pallas_call | solution.py:266
  152.9 0.3 collective-permute-start.9
  153.3 0.9 copy-done.10
  154.2 11.9 %dense_block.5 = (bf16[3,304,128]{2,1,0:T(8,128)(2,1)}, bf16[3,304,128]{2,1,0:T(8,128)(2,1)}, bf16[128,3584]{1,0:T(8,128)(2,1)}) custom-call(s32[1]{0:T(128)} %bitcast.4.core_ref, bf16[2,128,3584]{2,1,0:T(8,128)(2,1)} %copy-done.10, bf16[608,3584]{1,0:T(8,128)(2,1)} %refs_1_.3, bf16[608,3584]{1,0:T(8,128)(2,1)} %refs_2_.5, ...), custom_call_target="tpu_custom_call" | custom-call | flops 2789212160 | bytes 16293888 | tf_op jit(solution)/shard_map/dense_block/pallas_call | solution.py:183
  166.1 1.6 collective-permute-start.11
  167.6 1.7 collective-permute-done.8.refs_5_
  169.3 0.7 copy-done.13
  170.0 0.7 copy-done.11
  170.7 7.5 %weight_terms.4 = bf16[3,160,1792]{2,1,0:T(8,128)(2,1)} custom-call(s32[2]{0:T(128)} %get-tuple-element.76.tile_ref, bf16[3,304,128]{2,1,0:T(8,128)(2,1)} %get-tuple-element.77.refs_0_, bf16[3,304,128]{2,1,0:T(8,128)(2,1)} %copy-done.12, bf16[3,304,256]{2,1,0:T(8,128)(2,1)} %get-tuple-element.95.refs_2_, ...), custom_call_target="tpu_custom_call" | custom-call | flops 1761607680 | bytes 10928128 | tf_op jit(solution)/shard_map/weight_terms/pallas_call | solution.py:364
  178.2 1.5 collective-permute-start.10
  179.7 7.0 %weight_terms.5 = bf16[3,144,1792]{2,1,0:T(8,128)(2,1)} custom-call(s32[2]{0:T(128)} %get-tuple-element.106.tile_ref, bf16[3,304,128]{2,1,0:T(8,128)(2,1)} %get-tuple-element.77.refs_0_, bf16[3,304,128]{2,1,0:T(8,128)(2,1)} %copy-done.12, bf16[3,304,256]{2,1,0:T(8,128)(2,1)} %get-tuple-element.95.refs_2_, ...), custom_call_target="tpu_custom_call" | custom-call | flops 1585446912 | bytes 10756096 | tf_op jit(solution)/shard_map/weight_terms/pallas_call | solution.py:364
  186.6 2.3 collective-permute-done.11
  189.0 1.4 collective-permute-start.12
  190.4 2.3 add_convert_fusion.1
  192.7 3.4 %collective-permute-start.14 = (bf16[128,3584]{1,0:T(8,128)(2,1)}, bf16[128,3584]{1,0:T(8,128)(2,1)}, u32[]{:S(2)}, u32[]{:S(2)}) collective-permute-start(bf16[128,3584]{1,0:T(8,128)(2,1)} %add_convert_fusion.1), channel_id=1, source_target_pairs={{0,24},{8,16},{16,8},{24,0},{1,25},{9,17},{17,9},{25,1},{2,26},{10... | collective-permute-start | bytes 2752520 | tf_op jit(solution)/shard_map/ppermute | solution.py:454
  196.0 7.2 %weight_terms.7.refs_3_ = bf16[3,144,1792]{2,1,0:T(8,128)(2,1)} custom-call(s32[2]{0:T(128)} %get-tuple-element.112.tile_ref, bf16[3,304,128]{2,1,0:T(8,128)(2,1)} %get-tuple-element.77.refs_0_, bf16[3,304,128]{2,1,0:T(8,128)(2,1)} %copy-done.12, bf16[3,304,256]{2,1,0:T(8,128)(2,1)} %get-tuple-element.95.refs_2_, ...), custom_call_target="tpu_custom_call" | custom-call | flops 1585446912 | bytes 10756096 | tf_op jit(solution)/shard_map/weight_terms/pallas_call | solution.py:364
  203.2 7.3 %weight_terms.6.refs_0_ = bf16[3,160,1792]{2,1,0:T(8,128)(2,1)} custom-call(s32[2]{0:T(128)} %get-tuple-element.111.tile_ref, bf16[3,304,128]{2,1,0:T(8,128)(2,1)} %get-tuple-element.77.refs_0_, bf16[3,304,128]{2,1,0:T(8,128)(2,1)} %copy-done.12, bf16[3,304,256]{2,1,0:T(8,128)(2,1)} %get-tuple-element.95.refs_2_, ...), custom_call_target="tpu_custom_call" | custom-call | flops 1761607680 | bytes 10928128 | tf_op jit(solution)/shard_map/weight_terms/pallas_call | solution.py:364
  210.5 18.5 %reduce-scatter.2.cloned.1.call-done = bf16[16,3584]{1,0:T(8,128)(2,1)} async-done(((bf16[128,3584]{1,0:T(8,128)(2,1)}), bf16[16,3584]{1,0:T(8,128)(2,1)}) %reduce-scatter.2.cloned.1.call-update) | async-done | bytes 114704 | tf_op jit(solution)/shard_map/reduce_scatter | solution.py:495
  229.1 2.9 %add_convert_fusion.2 = bf16[3,160,896]{2,1,0:T(8,128)(2,1)} fusion(bf16[3,160,1792]{2,1,0:T(8,128)(2,1)S(1)} %collective-permute-done.10.refs_1_, bf16[3,160,1792]{2,1,0:T(8,128)(2,1)} %weight_terms.6.refs_0_), kind=kLoop, calls=%fused_computation.4 | loop fusion | flops 1720320 | bytes 2580480 | tf_op jit(solution)/shard_map/convert_element_type | solution.py:460
  232.0 1.1 collective-permute-start.15
  233.0 1.5 collective-permute-start.13
  234.5 2.2 add_convert_fusion.3
  236.7 1.0 collective-permute-start.16
  237.7 0.7 reshape.108
  238.4 3.7 %all-to-all-start.1 = ((bf16[4,4,3584]{2,1,0:T(4,128)(2,1)}), bf16[4,4,3584]{2,1,0:T(4,128)(2,1)S(1)}, u32[]{:S(2)}, u32[]{:S(2)}) async-start(bf16[4,4,3584]{2,1,0:T(4,128)(2,1)} %reshape.108), calls=%async_computation.2 | async-start | bytes 229376 | tf_op jit(solution)/shard_map/all_to_all | solution.py:78
  242.1 15.9 %all-to-all-done.1 = bf16[4,4,3584]{2,1,0:T(4,128)(2,1)S(1)} async-done(((bf16[4,4,3584]{2,1,0:T(4,128)(2,1)}), bf16[4,4,3584]{2,1,0:T(4,128)(2,1)S(1)}, u32[]{:S(2)}, u32[]{:S(2)}) %all-to-all-start.1) | async-done | bytes 114720 | tf_op jit(solution)/shard_map/all_to_all | solution.py:78
  258.0 0.5 convolution_bitcast_fusion
  258.5 1.5 copy-done.3
  260.0 2.9 %final_sum.1 = (bf16[3,304,448]{2,1,0:T(8,128)(2,1)S(1)}, bf16[3,304,448]{2,1,0:T(8,128)(2,1)S(1)}) custom-call(s32[1]{0:T(128)} %bitcast.4.core_ref, bf16[3,160,1792]{2,1,0:T(8,128)(2,1)S(1)} %copy-done, bf16[3,160,1792]{2,1,0:T(8,128)(2,1)S(1)} %copy-done.3, bf16[3,160,896]{2,1,0:T(8,128)(2,1)} %collective-permute-done.15.refs_2_, ...), custom_call_target="tpu_custom_call" | custom-call | flops 2451456 | bytes 6537216 | tf_op jit(solution)/shard_map/final_sum/pallas_call | solution.py:303
  263.0 3.0 %add_convert_fusion = bf16[128,3584]{1,0:T(8,128)(2,1)} fusion(f32[128,3584]{1,0:T(8,128)S(1)} %convolution_bitcast_fusion, bf16[128,3584]{1,0:T(8,128)(2,1)} %collective-permute-done.14, bf16[128,3584]{1,0:T(8,128)(2,1)} %collective-permute-done.13, bf16[128,3584]{1,0:T(8,128)(2,1)S(1)} %copy-done.15), kind=kLoop, calls=%fused_computation.2 | loop fusion | flops 3211264 | bytes 5505024 | tf_op jit(solution)/shard_map/convert_element_type | solution.py:526
  266.0 0.9 copy-done.14
  266.9 2.9 %join_halves.1 = (bf16[448,608]{1,0:T(8,128)(2,1)}, bf16[448,608]{1,0:T(8,128)(2,1)}, bf16[448,608]{1,0:T(8,128)(2,1)}) custom-call(s32[1]{0:T(128)} %bitcast.4.core_ref, bf16[3,304,448]{2,1,0:T(8,128)(2,1)} %copy-done.6, bf16[3,304,448]{2,1,0:T(8,128)(2,1)} %copy-done.14), custom_call_target="tpu_custom_call" | custom-call | bytes 3268608 | tf_op jit(solution)/shard_map/join_halves/pallas_call | solution.py:329
  (70 shorter events, 1.2 us)
Async XLA Ops:
  7.2 43.8 %all-gather.4.cloned.1.call-start = ((), (), s32[]{:S(2)}) async-start(), calls=%async_computation.3 | async-start | bytes 5160960 | tf_op jit(solution)/shard_map/all_gather | solution.py:448
  7.9 7.5 %copy-start.4 = (bf16[128,3584]{1,0:T(8,128)(2,1)S(1)}, bf16[128,3584]{1,0:T(8,128)(2,1)}, u32[]{:S(2)}) copy-start(bf16[128,3584]{1,0:T(8,128)(2,1)} %rows.1) | copy-start | bytes 2752516
  7.9 7.4 %copy-start.5 = (bf16[128,3584]{1,0:T(8,128)(2,1)S(1)}, bf16[128,3584]{1,0:T(8,128)(2,1)}, u32[]{:S(2)}) copy-start(bf16[128,3584]{1,0:T(8,128)(2,1)} %cots.1) | copy-start | bytes 2752516
  7.9 7.4 %copy-start.7 = (s32[128,2]{0,1:T(2,128)S(1)}, s32[128,2]{0,1:T(2,128)}, u32[]{:S(2)}) copy-start(s32[128,2]{0,1:T(2,128)} %param.12) | copy-start | bytes 3076
  7.9 7.4 %copy-start.8 = (f32[128,2]{0,1:T(2,128)S(1)}, f32[128,2]{0,1:T(2,128)}, u32[]{:S(2)}) copy-start(f32[128,2]{0,1:T(2,128)} %param.13) | copy-start | bytes 3076
  9.7 13.3 %copy-start.9 = (bf16[2,128,3584]{2,1,0:T(8,128)(2,1)}, bf16[2,128,3584]{2,1,0:T(8,128)(2,1)S(1)}, u32[]{:S(2)}) copy-start(bf16[2,128,3584]{2,1,0:T(8,128)(2,1)S(1)} %pad_maximum_fusion.refs_0_.refs_6_) | copy-start | bytes 5505028
  9.7 91.2 %collective-permute-start.1 = (bf16[2,128,3584]{2,1,0:T(8,128)(2,1)S(1)}, bf16[2,128,3584]{2,1,0:T(8,128)(2,1)}, u32[]{:S(2)}, u32[]{:S(2)}) collective-permute-start(bf16[2,128,3584]{2,1,0:T(8,128)(2,1)S(1)} %pad_maximum_fusion.refs_0_.refs_6_), channel_id=1, source_target_pairs={{0,1},{1,0},{2,3},{3,2},{4,5},{5,4},{6,7},{7,6},{8,9},{9,8},{10,11... | collective-permute-start | bytes 5505032 | tf_op jit(solution)/shard_map/ppermute | solution.py:457
  10.2 90.7 %collective-permute-start.3 = (bf16[2,128,3584]{2,1,0:T(8,128)(2,1)S(1)}, bf16[2,128,3584]{2,1,0:T(8,128)(2,1)}, u32[]{:S(2)}, u32[]{:S(2)}) collective-permute-start(bf16[2,128,3584]{2,1,0:T(8,128)(2,1)S(1)} %pad_maximum_fusion.refs_0_.refs_6_), channel_id=1, source_target_pairs={{0,8},{8,0},{16,24},{24,16},{1,9},{9,1},{17,25},{25,17},{2,10},{10... | collective-permute-start | bytes 5505032 | tf_op jit(solution)/shard_map/ppermute | solution.py:451
  12.9 88.1 %collective-permute-start.2 = (bf16[2,128,3584]{2,1,0:T(8,128)(2,1)S(1)}, bf16[2,128,3584]{2,1,0:T(8,128)(2,1)}, u32[]{:S(2)}, u32[]{:S(2)}) collective-permute-start(bf16[2,128,3584]{2,1,0:T(8,128)(2,1)S(1)} %pad_maximum_fusion.refs_0_.refs_6_), channel_id=1, source_target_pairs={{0,24},{8,16},{16,8},{24,0},{1,25},{9,17},{17,9},{25,1},{2,26},{10... | collective-permute-start | bytes 5505032 | tf_op jit(solution)/shard_map/ppermute | solution.py:454
  16.6 83.5 %all-to-all-start = ((bf16[4,8,3584]{2,1,0:T(8,128)(2,1)}), bf16[4,8,3584]{2,1,0:T(8,128)(2,1)S(1)}, u32[]{:S(2)}, u32[]{:S(2)}) async-start(bf16[4,8,3584]{2,1,0:T(8,128)(2,1)} %bitcast.2), calls=%async_computation | async-start | bytes 458752 | tf_op jit(solution)/shard_map/all_to_all | solution.py:470
  20.0 108.3 %all-gather.6.cloned.1.call-start = ((), (), s32[]{:S(2)}) async-start(), calls=%async_computation.5 | async-start | bytes 2064384 | tf_op jit(solution)/shard_map/all_gather | solution.py:485
  62.9 38.0 %collective-permute-start = (bf16[3,304,128]{2,1,0:T(8,128)(2,1)}, bf16[3,304,128]{2,1,0:T(8,128)(2,1)S(1)}, u32[]{:S(2)}, u32[]{:S(2)}) collective-permute-start(bf16[3,304,128]{2,1,0:T(8,128)(2,1)} %get-tuple-element.74), channel_id=1, source_target_pairs={{0,1},{1,0},{2,3},{3,2},{4,5},{5,4},{6,7},{7,6},{8,9},{9,8},{10,11... | collective-permute-start | bytes 700424 | tf_op jit(solution)/shard_map/ppermute | solution.py:457
  100.9 16.9 %copy-start.12 = (bf16[3,304,128]{2,1,0:T(8,128)(2,1)}, bf16[3,304,128]{2,1,0:T(8,128)(2,1)S(1)}, u32[]{:S(2)}) copy-start(bf16[3,304,128]{2,1,0:T(8,128)(2,1)S(1)} %collective-permute-done.refs_1_) | copy-start | bytes 700420
  101.0 128.1 %reduce-scatter.2.cloned.1.call-start = ((), (), s32[]{:S(2)}) async-start(), calls=%async_computation.4 | async-start | bytes 1032192 | tf_op jit(solution)/shard_map/reduce_scatter | solution.py:495
  101.2 18.9 %collective-permute-start.6 = (bf16[2,128,3584]{2,1,0:T(8,128)(2,1)}, bf16[2,128,3584]{2,1,0:T(8,128)(2,1)}, u32[]{:S(2)}, u32[]{:S(2)}) collective-permute-start(bf16[2,128,3584]{2,1,0:T(8,128)(2,1)} %collective-permute-done.3.refs_0_.refs_8_), channel_id=1, source_target_pairs={{0,1},{1,0},{2,3},{3,2},{4,5},{5,4},{6,7},{7,6},{8,9},{9,8},{10,11... | collective-permute-start | bytes 5505032 | tf_op jit(solution)/shard_map/ppermute | solution.py:457
  101.3 18.8 %collective-permute-start.7 = (bf16[2,128,3584]{2,1,0:T(8,128)(2,1)}, bf16[2,128,3584]{2,1,0:T(8,128)(2,1)}, u32[]{:S(2)}, u32[]{:S(2)}) collective-permute-start(bf16[2,128,3584]{2,1,0:T(8,128)(2,1)} %collective-permute-done.2.refs_1_.refs_9_), channel_id=1, source_target_pairs={{0,1},{1,0},{2,3},{3,2},{4,5},{5,4},{6,7},{7,6},{8,9},{9,8},{10,11... | collective-permute-start | bytes 5505032 | tf_op jit(solution)/shard_map/ppermute | solution.py:457
  101.8 51.1 %collective-permute-start.4 = (bf16[2,128,3584]{2,1,0:T(8,128)(2,1)}, bf16[2,128,3584]{2,1,0:T(8,128)(2,1)S(1)}, u32[]{:S(2)}, u32[]{:S(2)}) collective-permute-start(bf16[2,128,3584]{2,1,0:T(8,128)(2,1)} %collective-permute-done.2.refs_1_.refs_9_), channel_id=1, source_target_pairs={{0,8},{8,0},{16,24},{24,16},{1,9},{9,1},{17,25},{25,17},{2,10},{10... | collective-permute-start | bytes 5505032 | tf_op jit(solution)/shard_map/ppermute | solution.py:451
  117.9 2.2 collective-permute-start.5
  152.9 1.2 copy-start.10
  152.9 16.4 %collective-permute-start.9 = (bf16[2,128,3584]{2,1,0:T(8,128)(2,1)S(1)}, bf16[2,128,3584]{2,1,0:T(8,128)(2,1)S(1)}, u32[]{:S(2)}, u32[]{:S(2)}) collective-permute-start(bf16[2,128,3584]{2,1,0:T(8,128)(2,1)S(1)} %collective-permute-done.4.refs_0_.refs_12_), channel_id=1, source_target_pairs={{0,1},{1,0},{2,3},{3,2},{4,5},{5,4},{6,7},{7,6},{8,9},{9,8},{10,11... | collective-permute-start | bytes 5505032 | tf_op jit(solution)/shard_map/ppermute | solution.py:457
  166.1 22.9 %collective-permute-start.11 = (bf16[128,3584]{1,0:T(8,128)(2,1)}, bf16[128,3584]{1,0:T(8,128)(2,1)}, u32[]{:S(2)}, u32[]{:S(2)}) collective-permute-start(bf16[128,3584]{1,0:T(8,128)(2,1)} %get-tuple-element.109), channel_id=1, source_target_pairs={{0,8},{8,0},{16,24},{24,16},{1,9},{9,1},{17,25},{25,17},{2,10},{10... | collective-permute-start | bytes 2752520 | tf_op jit(solution)/shard_map/ppermute | solution.py:451
  167.6 1.7 collective-permute-start.8
  169.3 0.7 copy-start.13
  169.3 1.3 copy-start.11
  178.2 12.2 %copy-start.16 = (bf16[128,3584]{1,0:T(8,128)(2,1)S(1)}, bf16[128,3584]{1,0:T(8,128)(2,1)}, u32[]{:S(2)}) copy-start(bf16[128,3584]{1,0:T(8,128)(2,1)} %get-tuple-element.119) | copy-start | bytes 2752516
  178.2 50.9 %collective-permute-start.10 = (bf16[3,160,1792]{2,1,0:T(8,128)(2,1)}, bf16[3,160,1792]{2,1,0:T(8,128)(2,1)S(1)}, u32[]{:S(2)}, u32[]{:S(2)}) collective-permute-start(bf16[3,160,1792]{2,1,0:T(8,128)(2,1)} %weight_terms.4), channel_id=1, source_target_pairs={{0,2},{1,3},{2,0},{3,1},{4,6},{5,7},{6,4},{7,5},{8,10},{9,11},{10,... | collective-permute-start | bytes 5160968 | tf_op jit(solution)/shard_map/ppermute | solution.py:457
  189.0 40.1 %collective-permute-start.12 = (bf16[3,144,1792]{2,1,0:T(8,128)(2,1)}, bf16[3,144,1792]{2,1,0:T(8,128)(2,1)}, u32[]{:S(2)}, u32[]{:S(2)}) collective-permute-start(bf16[3,144,1792]{2,1,0:T(8,128)(2,1)} %weight_terms.5), channel_id=1, source_target_pairs={{0,4},{1,5},{2,6},{3,7},{4,0},{5,1},{6,2},{7,3},{8,12},{9,13},{10,... | collective-permute-start | bytes 4644872 | tf_op jit(solution)/shard_map/ppermute | solution.py:457
  192.7 45.1 %collective-permute-start.14 = (bf16[128,3584]{1,0:T(8,128)(2,1)}, bf16[128,3584]{1,0:T(8,128)(2,1)}, u32[]{:S(2)}, u32[]{:S(2)}) collective-permute-start(bf16[128,3584]{1,0:T(8,128)(2,1)} %add_convert_fusion.1), channel_id=1, source_target_pairs={{0,24},{8,16},{16,8},{24,0},{1,25},{9,17},{17,9},{25,1},{2,26},{10... | collective-permute-start | bytes 2752520 | tf_op jit(solution)/shard_map/ppermute | solution.py:454
  210.5 24.0 %copy-start.1 = (bf16[3,144,1792]{2,1,0:T(8,128)(2,1)S(1)}, bf16[3,144,1792]{2,1,0:T(8,128)(2,1)}, u32[]{:S(2)}) copy-start(bf16[3,144,1792]{2,1,0:T(8,128)(2,1)} %weight_terms.7.refs_3_) | copy-start | bytes 4644868
  229.1 8.7 %copy-start.18 = (bf16[16,3584]{1,0:T(8,128)(2,1)S(1)}, bf16[16,3584]{1,0:T(8,128)(2,1)}, u32[]{:S(2)}) copy-start(bf16[16,3584]{1,0:T(8,128)(2,1)} %reduce-scatter.2.cloned.1.call-done) | copy-start | bytes 344068
  229.1 5.5 %copy-start.2 = (bf16[3,160,1792]{2,1,0:T(8,128)(2,1)}, bf16[3,160,1792]{2,1,0:T(8,128)(2,1)S(1)}, u32[]{:S(2)}) copy-start(bf16[3,160,1792]{2,1,0:T(8,128)(2,1)S(1)} %collective-permute-done.10.refs_1_) | copy-start | bytes 5160964
  232.0 10.1 %copy-start.17 = (bf16[128,16]{1,0:T(8,128)(2,1)S(1)}, bf16[128,16]{1,0:T(8,128)(2,1)}, u32[]{:S(2)}) copy-start(bf16[128,16]{1,0:T(8,128)(2,1)} %fusion.1) | copy-start | bytes 12292
  232.0 26.5 %collective-permute-start.15 = (bf16[3,160,896]{2,1,0:T(8,128)(2,1)}, bf16[3,160,896]{2,1,0:T(8,128)(2,1)}, u32[]{:S(2)}, u32[]{:S(2)}) collective-permute-start(bf16[3,160,896]{2,1,0:T(8,128)(2,1)} %add_convert_fusion.2), channel_id=1, source_target_pairs={{0,4},{1,5},{2,6},{3,7},{4,0},{5,1},{6,2},{7,3},{8,12},{9,13},{10,... | collective-permute-start | bytes 2580488 | tf_op jit(solution)/shard_map/ppermute | solution.py:457
  233.0 29.9 %collective-permute-start.13 = (bf16[128,3584]{1,0:T(8,128)(2,1)}, bf16[128,3584]{1,0:T(8,128)(2,1)}, u32[]{:S(2)}, u32[]{:S(2)}) collective-permute-start(bf16[128,3584]{1,0:T(8,128)(2,1)} %get-tuple-element.118), channel_id=1, source_target_pairs={{0,8},{8,0},{16,24},{24,16},{1,9},{9,1},{17,25},{25,17},{2,10},{10... | collective-permute-start | bytes 2752520 | tf_op jit(solution)/shard_map/ppermute | solution.py:451
  236.7 21.8 %copy-start = (bf16[3,160,1792]{2,1,0:T(8,128)(2,1)S(1)}, bf16[3,160,1792]{2,1,0:T(8,128)(2,1)}, u32[]{:S(2)}) copy-start(bf16[3,160,1792]{2,1,0:T(8,128)(2,1)} %weight_terms.6.refs_0_) | copy-start | bytes 5160964
  236.7 21.8 %collective-permute-start.16 = (bf16[3,144,896]{2,1,0:T(8,128)(2,1)}, bf16[3,144,896]{2,1,0:T(8,128)(2,1)}, u32[]{:S(2)}, u32[]{:S(2)}) collective-permute-start(bf16[3,144,896]{2,1,0:T(8,128)(2,1)} %add_convert_fusion.3), channel_id=1, source_target_pairs={{0,2},{1,3},{2,0},{3,1},{4,6},{5,7},{6,4},{7,5},{8,10},{9,11},{10,... | collective-permute-start | bytes 2322440 | tf_op jit(solution)/shard_map/ppermute | solution.py:457
  238.4 19.6 %all-to-all-start.1 = ((bf16[4,4,3584]{2,1,0:T(4,128)(2,1)}), bf16[4,4,3584]{2,1,0:T(4,128)(2,1)S(1)}, u32[]{:S(2)}, u32[]{:S(2)}) async-start(bf16[4,4,3584]{2,1,0:T(4,128)(2,1)} %reshape.108), calls=%async_computation.2 | async-start | bytes 229376 | tf_op jit(solution)/shard_map/all_to_all | solution.py:78
  258.0 5.0 %copy-start.15 = (bf16[128,3584]{1,0:T(8,128)(2,1)S(1)}, bf16[128,3584]{1,0:T(8,128)(2,1)}, u32[]{:S(2)}) copy-start(bf16[128,3584]{1,0:T(8,128)(2,1)} %get-tuple-element.75) | copy-start | bytes 2752516
  258.5 1.5 copy-start.3
  262.9 3.1 %copy-start.6 = (bf16[3,304,448]{2,1,0:T(8,128)(2,1)}, bf16[3,304,448]{2,1,0:T(8,128)(2,1)S(1)}, u32[]{:S(2)}) copy-start(bf16[3,304,448]{2,1,0:T(8,128)(2,1)S(1)} %get-tuple-element.129.mine) | copy-start | bytes 2451460
  262.9 3.1 %collective-permute-start.17 = (bf16[3,304,448]{2,1,0:T(8,128)(2,1)S(1)}, bf16[3,304,448]{2,1,0:T(8,128)(2,1)S(1)}, u32[]{:S(2)}, u32[]{:S(2)}) collective-permute-start(bf16[3,304,448]{2,1,0:T(8,128)(2,1)S(1)} %get-tuple-element.130), channel_id=1, source_target_pairs={{0,1},{1,0},{2,3},{3,2},{4,5},{5,4},{6,7},{7,6},{8,9},{9,8},{10,11... | collective-permute-start | bytes 2451464 | tf_op jit(solution)/shard_map/ppermute | solution.py:457
  266.0 0.9 copy-start.14
Sparse Core Ops, SparseCore 0:
  9.9 41.0 all-gather.3
  101.1 27.0 all-gather.5
  190.5 38.5 reduce-scatter.1

commit v2 on v0

--- a/solution.py
+++ b/solution.py
@@ -506,19 +506,18 @@
     low_near, high_near = across(low_sent, 2), across(high_sent, 4)
     from_pair = pairs(paired_partial)
     low_kept, high_kept, from_pair, routed = together(low_kept, high_kept, from_pair, routed)
-    back = slots_back(routed, experts)
-    from_last, back = together(from_last, back)
     from_mirror = mirror(add(mirrored_partial, from_last))
-    low_near, high_near, low_kept, high_kept, back = together(
-        low_near, high_near, low_kept, high_kept, back
+    low_near, high_near, low_kept, high_kept = together(
+        low_near, high_near, low_kept, high_kept
     )
     low_far = across(add(low_kept[:, :, :width], low_near[:, :, :width]), 4)
     high_far = across(add(high_kept[:, :, :width], high_near[:, :, :width]), 2)
     low_far, high_far, from_mirror = together(low_far, high_far, from_mirror)
-    routed_input = to_tokens(back, dispatch, me, experts)
     mine, other = final_sum(
         core, (low_kept, low_near, low_far), (high_kept, high_near, high_far)
     )
+    mine, routed = together(mine, routed)
+    routed_input = to_tokens(slots_back(routed, experts), dispatch, me, experts)
     grads = join_halves(core, mine, across(other, 1))
     grad_input = (
         partial0.astype(F32)

time: 279 us -> 282 us (1.011)
  the two profiles are of different devices: /device:TPU:9 before, /device:TPU:0 now
where the time goes in v2:
time: 282 us; the launch traced here: 281 us
  waiting for transfers between devices  120 us (43%)
  Pallas kernels  101 us (36%)
  starting transfers between devices  25.9 us (9%)
  between operations  14.1 us (5%)
  other arithmetic  11.7 us (4%)
  local copies, waits for them, and re-layouts  8.4 us (3%)
    pallas_call x3, Pallas kernels, dense_block(): pl.pallas_call(kernel, in_specs=[pl.BlockSpec(memory_space=pltpu.SMEM)] +...  39.7 us
    all_to_all x1, waiting for transfers between devices, line_body(): got = lax.all_to_all(sent, 'tp', split_axis=0, concat_axis=0, tiled=True)  36 us
    pallas_call x4, Pallas kernels, weight_terms(): pl.pallas_call(kernel, grid_spec=pltpu.PrefetchScalarGridSpec(num_scalar_...  29.1 us
    all_gather x1, waiting for transfers between devices, line_body(): down = lax.all_gather(dense_down.T, 'ep', axis=0, tiled=True)  26.3 us
    pallas_call x1, Pallas kernels, expert_block(): pl.pallas_call(kernel, in_specs=[vmem, hbm, hbm, hbm], out_specs=[hbm, hb...  24.7 us
    ppermute x12, waiting for transfers between devices, across(): return lax.ppermute(value, 'ep', [(i, i ^ apart) for i in range(8)])  21.3 us
    reduce_scatter x1, waiting for transfers between devices, line_body(): routed = lax.psum_scatter(slot_terms, 'ep', scatter_dimension=0, tiled=True)  16.1 us
    all_gather x1, waiting for transfers between devices, line_body(): slots = lax.all_gather(got, 'ep', axis=0, tiled=False)  8.26 us
  transfers between devices with their start and end apart: 23, of which 11 were waited for; matrix products, arithmetic and copies ran while one was open for 6% of the time, Pallas kernels for 34%

profile of v2, /device:TPU:0, one launch (start us, length us, event | category | flops | bytes accessed | tf_op | source)
XLA Modules:
  0.0 281.4 jit_solution(12323496897240522881)
XLA Ops:
  7.2 0.7 all-gather.4.cloned.1.call-update
  7.9 1.8 pad_maximum_fusion.refs_0_.refs_6_
  9.7 0.5 collective-permute-start.1
  10.2 2.7 collective-permute-start.3
  12.9 2.5 collective-permute-start.2
  15.4 1.2 routed_rows.1
  16.6 3.4 %all-to-all-start = ((bf16[4,8,3584]{2,1,0:T(8,128)(2,1)}), bf16[4,8,3584]{2,1,0:T(8,128)(2,1)S(1)}, u32[]{:S(2)}, u32[]{:S(2)}) async-start(bf16[4,8,3584]{2,1,0:T(8,128)(2,1)} %bitcast.2), calls=%async_computation | async-start | bytes 458752 | tf_op jit(solution)/shard_map/all_to_all | solution.py:470
  20.1 0.1 eq.56
  20.3 0.1 eq.52
  20.6 1.2 reduce-window.6
  22.2 0.1 copy.35
  22.5 0.1 copy.34
  22.6 0.3 eq.60
  23.0 0.3 eq.61
  23.3 0.3 mul.10
  23.7 0.3 mul.11
  24.0 0.7 pad_add_fusion
  24.7 26.3 %all-gather.4.cloned.1.call-done.refs_3_.refs_4_ = bf16[3584,608]{1,0:T(8,128)(2,1)} async-done(((bf16[448,608]{1,0:T(8,128)(2,1)}), bf16[3584,608]{1,0:T(8,128)(2,1)}) %all-gather.4.cloned.1.call-update) | async-done | bytes 4358160 | tf_op jit(solution)/shard_map/all_gather | solution.py:448
  51.0 11.9 %dense_block.3 = (bf16[3,304,128]{2,1,0:T(8,128)(2,1)}, bf16[3,304,128]{2,1,0:T(8,128)(2,1)}, bf16[128,3584]{1,0:T(8,128)(2,1)}) custom-call(s32[1]{0:T(128)} %bitcast.4.core_ref, bf16[2,128,3584]{2,1,0:T(8,128)(2,1)} %copy-done.8, bf16[608,3584]{1,0:T(8,128)(2,1)} %refs_1_.3, bf16[608,3584]{1,0:T(8,128)(2,1)} %refs_2_.5, ...), custom_call_target="tpu_custom_call" | custom-call | flops 2789212160 | bytes 16293888 | tf_op jit(solution)/shard_map/dense_block/pallas_call | solution.py:183
  62.9 0.3 collective-permute-start
  63.2 0.6 pad_add_fusion.2
  63.8 0.2 fusion.1
  64.0 36.0 %all-to-all-done = bf16[4,8,3584]{2,1,0:T(8,128)(2,1)S(1)} async-done(((bf16[4,8,3584]{2,1,0:T(8,128)(2,1)}), bf16[4,8,3584]{2,1,0:T(8,128)(2,1)S(1)}, u32[]{:S(2)}, u32[]{:S(2)}) %all-to-all-start) | async-done | bytes 229408 | tf_op jit(solution)/shard_map/all_to_all | solution.py:470
  100.2 0.7 reshape.104
  101.0 0.2 reduce-scatter.2.cloned.1.call-start
  101.3 0.5 collective-permute-start.7
  101.8 16.0 %dense_block.4 = (bf16[3,304,256]{2,1,0:T(8,128)(2,1)}, bf16[3,304,256]{2,1,0:T(8,128)(2,1)}, bf16[128,3584]{1,0:T(8,128)(2,1)}, bf16[128,3584]{1,0:T(8,128)(2,1)}) custom-call(s32[1]{0:T(128)} %bitcast.4.core_ref, bf16[2,128,3584]{2,1,0:T(8,128)(2,1)} %collective-permute-done.3.refs_0_.refs_8_, ...), custom_call_target="tpu_custom_call" | custom-call | flops 5578424320 | bytes 19513344 | tf_op jit(solution)/shard_map/dense_block/pallas_call | solution.py:183
  117.9 0.2 collective-permute-start.5
  118.0 1.9 collective-permute-done.5.refs_3_
  120.0 8.3 %all-gather.6.cloned.1.call-done = bf16[16,16,3584]{2,1,0:T(8,128)(2,1)} async-done(((bf16[2,16,3584]{2,1,0:T(8,128)(2,1)}), bf16[16,16,3584]{2,1,0:T(8,128)(2,1)}) %all-gather.6.cloned.1.call-update) | async-done | bytes 1835024 | tf_op jit(solution)/shard_map/all_gather | solution.py:485
  128.2 24.7 %expert_block.1 = (bf16[608,3584]{1,0:T(8,128)(2,1)}, bf16[608,3584]{1,0:T(8,128)(2,1)}, bf16[608,3584]{1,0:T(8,128)(2,1)}, bf16[128,3584]{1,0:T(8,128)(2,1)}) custom-call(bf16[8,2,16,3584]{3,2,1,0:T(8,128)(2,1)} %bitcast.49, bf16[608,3584]{1,0:T(8,128)(2,1)} %bitcast.46, bf16[608,3584]{1,0:T(8,128)(2,1)} %bitcast.47, bf16[608,3584]{1,0:T(8,128)(2,1)} %bitcast.48), custom_call_target="tpu_custom_call" | custom-call | flops 1 | bytes 1 | tf_op jit(solution)/shard_map/expert_block/pallas_call | solution.py:266
  153.0 0.3 collective-permute-start.9
  153.3 0.9 copy-done.9
  154.2 11.9 %dense_block.5 = (bf16[3,304,128]{2,1,0:T(8,128)(2,1)}, bf16[3,304,128]{2,1,0:T(8,128)(2,1)}, bf16[128,3584]{1,0:T(8,128)(2,1)}) custom-call(s32[1]{0:T(128)} %bitcast.4.core_ref, bf16[2,128,3584]{2,1,0:T(8,128)(2,1)} %copy-done.9, bf16[608,3584]{1,0:T(8,128)(2,1)} %refs_1_.3, bf16[608,3584]{1,0:T(8,128)(2,1)} %refs_2_.5, ...), custom_call_target="tpu_custom_call" | custom-call | flops 2789212160 | bytes 16293888 | tf_op jit(solution)/shard_map/dense_block/pallas_call | solution.py:183
  166.0 1.6 collective-permute-start.10
  167.6 1.7 collective-permute-done.8.refs_5_
  169.3 0.7 copy-done.12
  170.0 7.5 %weight_terms.7 = bf16[3,160,1792]{2,1,0:T(8,128)(2,1)} custom-call(s32[2]{0:T(128)} %get-tuple-element.108.tile_ref, bf16[3,304,128]{2,1,0:T(8,128)(2,1)} %get-tuple-element.79.refs_0_, bf16[3,304,128]{2,1,0:T(8,128)(2,1)} %copy-done.11, bf16[3,304,256]{2,1,0:T(8,128)(2,1)} %get-tuple-element.97.refs_2_, bf16[3,304,256]{2,1,0:T(8,128)(2,1)} %copy-done.10, ...), custom_call_target="tpu_custom_call" | custom-call | flops 1761607680 | bytes 10928128 | tf_op jit(solution)/shard_map/weight_terms/pallas_call | solution.py:364
  177.5 1.6 collective-permute-start.12
  179.0 7.0 %weight_terms.4 = bf16[3,144,1792]{2,1,0:T(8,128)(2,1)} custom-call(s32[2]{0:T(128)} %get-tuple-element.78.tile_ref, bf16[3,304,128]{2,1,0:T(8,128)(2,1)} %get-tuple-element.79.refs_0_, bf16[3,304,128]{2,1,0:T(8,128)(2,1)} %copy-done.11, bf16[3,304,256]{2,1,0:T(8,128)(2,1)} %get-tuple-element.97.refs_2_, bf16[3,304,256]{2,1,0:T(8,128)(2,1)} %copy-done.10, ...), custom_call_target="tpu_custom_call" | custom-call | flops 1585446912 | bytes 10756096 | tf_op jit(solution)/shard_map/weight_terms/pallas_call | solution.py:364
  186.0 2.8 collective-permute-done.10
  188.8 1.4 collective-permute-start.13
  190.3 1.5 collective-permute-start.11
  191.8 1.1 add_convert_fusion.1
  192.9 2.4 collective-permute-start.16
  195.3 7.2 %weight_terms.6.refs_3_ = bf16[3,144,1792]{2,1,0:T(8,128)(2,1)} custom-call(s32[2]{0:T(128)} %get-tuple-element.113.tile_ref, bf16[3,304,128]{2,1,0:T(8,128)(2,1)} %get-tuple-element.79.refs_0_, bf16[3,304,128]{2,1,0:T(8,128)(2,1)} %copy-done.11, bf16[3,304,256]{2,1,0:T(8,128)(2,1)} %get-tuple-element.97.refs_2_, bf16[3,304,256]{2,1,0:T(8,128)(2,1)} %copy-done.10, ...), custom_call_target="tpu_custom_call" | custom-call | flops 1585446912 | bytes 10756096 | tf_op jit(solution)/shard_map/weight_terms/pallas_call | solution.py:364
  202.5 7.4 %weight_terms.5.refs_0_ = bf16[3,160,1792]{2,1,0:T(8,128)(2,1)} custom-call(s32[2]{0:T(128)} %get-tuple-element.112.tile_ref, bf16[3,304,128]{2,1,0:T(8,128)(2,1)} %get-tuple-element.79.refs_0_, bf16[3,304,128]{2,1,0:T(8,128)(2,1)} %copy-done.11, bf16[3,304,256]{2,1,0:T(8,128)(2,1)} %get-tuple-element.97.refs_2_, bf16[3,304,256]{2,1,0:T(8,128)(2,1)} %copy-done.10, ...), custom_call_target="tpu_custom_call" | custom-call | flops 1761607680 | bytes 10928128 | tf_op jit(solution)/shard_map/weight_terms/pallas_call | solution.py:364
  209.9 3.0 %collective-permute-done.11 = bf16[128,3584]{1,0:T(8,128)(2,1)} collective-permute-done((bf16[128,3584]{1,0:T(8,128)(2,1)}, bf16[128,3584]{1,0:T(8,128)(2,1)}, u32[]{:S(2)}, u32[]{:S(2)}) %collective-permute-start.11) | collective-permute-done | bytes 917536 | tf_op jit(solution)/shard_map/ppermute | solution.py:451
  212.9 16.1 %reduce-scatter.2.cloned.1.call-done = bf16[16,3584]{1,0:T(8,128)(2,1)} async-done(((bf16[128,3584]{1,0:T(8,128)(2,1)}), bf16[16,3584]{1,0:T(8,128)(2,1)}) %reduce-scatter.2.cloned.1.call-update) | async-done | bytes 114704 | tf_op jit(solution)/shard_map/reduce_scatter | solution.py:495
  229.0 1.6 add_convert_fusion.2
  230.6 1.0 collective-permute-start.14
  231.7 1.3 add_convert_fusion.3
  233.0 1.1 collective-permute-start.15
  234.1 17.6 %collective-permute-done.15.refs_5_ = bf16[3,144,896]{2,1,0:T(8,128)(2,1)S(1)} collective-permute-done((bf16[3,144,896]{2,1,0:T(8,128)(2,1)S(1)}, bf16[3,144,896]{2,1,0:T(8,128)(2,1)S(1)}, u32[]{:S(2)}, u32[]{:S(2)}) %collective-permute-start.15) | collective-permute-done | bytes 774176 | tf_op jit(solution)/shard_map/ppermute | solution.py:457
  251.8 3.0 %final_sum.1 = (bf16[3,304,448]{2,1,0:T(8,128)(2,1)S(1)}, bf16[3,304,448]{2,1,0:T(8,128)(2,1)S(1)}) custom-call(s32[1]{0:T(128)} %bitcast.4.core_ref, bf16[3,160,1792]{2,1,0:T(8,128)(2,1)S(1)} %copy-done, bf16[3,160,1792]{2,1,0:T(8,128)(2,1)} %collective-permute-done.12.refs_1_, bf16[3,160,896]{2,1,0:T(8,128)(2,1)S(1)} %collective-permute-done.14.refs_2_, ...), custom_call_target="tpu_custom_call" | custom-call | flops 2451456 | bytes 6537216 | tf_op jit(solution)/shard_map/final_sum/pallas_call | solution.py:303
  254.7 0.9 copy-done.4
  255.7 0.9 copy-done.7
  256.6 0.7 reshape.108
  257.3 4.6 %all-to-all-start.1 = ((bf16[4,4,3584]{2,1,0:T(4,128)(2,1)}), bf16[4,4,3584]{2,1,0:T(4,128)(2,1)S(1)}, u32[]{:S(2)}, u32[]{:S(2)}) async-start(bf16[4,4,3584]{2,1,0:T(4,128)(2,1)} %reshape.108), calls=%async_computation.2 | async-start | bytes 229376 | tf_op jit(solution)/shard_map/all_to_all | solution.py:78
  262.0 5.8 %all-to-all-done.1 = bf16[4,4,3584]{2,1,0:T(4,128)(2,1)S(1)} async-done(((bf16[4,4,3584]{2,1,0:T(4,128)(2,1)}), bf16[4,4,3584]{2,1,0:T(4,128)(2,1)S(1)}, u32[]{:S(2)}, u32[]{:S(2)}) %all-to-all-start.1) | async-done | bytes 114720 | tf_op jit(solution)/shard_map/all_to_all | solution.py:78
  267.8 0.5 convolution_bitcast_fusion
  268.3 2.8 %add_convert_fusion = bf16[128,3584]{1,0:T(8,128)(2,1)} fusion(f32[128,3584]{1,0:T(8,128)S(1)} %convolution_bitcast_fusion, bf16[128,3584]{1,0:T(8,128)(2,1)} %collective-permute-done.16, bf16[128,3584]{1,0:T(8,128)(2,1)} %collective-permute-done.11, bf16[128,3584]{1,0:T(8,128)(2,1)S(1)} %copy-done.14), kind=kLoop, calls=%fused_computation.2 | loop fusion | flops 3211264 | bytes 5505024 | tf_op jit(solution)/shard_map/convert_element_type | solution.py:527
  271.1 0.9 copy-done.13
  272.0 2.9 %join_halves.1 = (bf16[448,608]{1,0:T(8,128)(2,1)}, bf16[448,608]{1,0:T(8,128)(2,1)}, bf16[448,608]{1,0:T(8,128)(2,1)}) custom-call(s32[1]{0:T(128)} %bitcast.4.core_ref, bf16[3,304,448]{2,1,0:T(8,128)(2,1)} %copy-done.4, bf16[3,304,448]{2,1,0:T(8,128)(2,1)} %copy-done.13), custom_call_target="tpu_custom_call" | custom-call | bytes 3268608 | tf_op jit(solution)/shard_map/join_halves/pallas_call | solution.py:329
  (66 shorter events, 1.5 us)
Async XLA Ops:
  7.2 43.8 %all-gather.4.cloned.1.call-start = ((), (), s32[]{:S(2)}) async-start(), calls=%async_computation.3 | async-start | bytes 5160960 | tf_op jit(solution)/shard_map/all_gather | solution.py:448
  7.9 7.5 %copy-start.2 = (bf16[128,3584]{1,0:T(8,128)(2,1)S(1)}, bf16[128,3584]{1,0:T(8,128)(2,1)}, u32[]{:S(2)}) copy-start(bf16[128,3584]{1,0:T(8,128)(2,1)} %rows.1) | copy-start | bytes 2752516
  7.9 7.4 %copy-start.3 = (bf16[128,3584]{1,0:T(8,128)(2,1)S(1)}, bf16[128,3584]{1,0:T(8,128)(2,1)}, u32[]{:S(2)}) copy-start(bf16[128,3584]{1,0:T(8,128)(2,1)} %cots.1) | copy-start | bytes 2752516
  7.9 7.4 %copy-start.5 = (s32[128,2]{0,1:T(2,128)S(1)}, s32[128,2]{0,1:T(2,128)}, u32[]{:S(2)}) copy-start(s32[128,2]{0,1:T(2,128)} %param.12) | copy-start | bytes 3076
  7.9 7.4 %copy-start.6 = (f32[128,2]{0,1:T(2,128)S(1)}, f32[128,2]{0,1:T(2,128)}, u32[]{:S(2)}) copy-start(f32[128,2]{0,1:T(2,128)} %param.13) | copy-start | bytes 3076
  9.7 13.3 %copy-start.8 = (bf16[2,128,3584]{2,1,0:T(8,128)(2,1)}, bf16[2,128,3584]{2,1,0:T(8,128)(2,1)S(1)}, u32[]{:S(2)}) copy-start(bf16[2,128,3584]{2,1,0:T(8,128)(2,1)S(1)} %pad_maximum_fusion.refs_0_.refs_6_) | copy-start | bytes 5505028
  9.7 91.2 %collective-permute-start.1 = (bf16[2,128,3584]{2,1,0:T(8,128)(2,1)S(1)}, bf16[2,128,3584]{2,1,0:T(8,128)(2,1)}, u32[]{:S(2)}, u32[]{:S(2)}) collective-permute-start(bf16[2,128,3584]{2,1,0:T(8,128)(2,1)S(1)} %pad_maximum_fusion.refs_0_.refs_6_), channel_id=1, source_target_pairs={{0,1},{1,0},{2,3},{3,2},{4,5},{5,4},{6,7},{7,6},{8,9},{9,8},{10,11... | collective-permute-start | bytes 5505032 | tf_op jit(solution)/shard_map/ppermute | solution.py:457
  10.2 90.7 %collective-permute-start.3 = (bf16[2,128,3584]{2,1,0:T(8,128)(2,1)S(1)}, bf16[2,128,3584]{2,1,0:T(8,128)(2,1)}, u32[]{:S(2)}, u32[]{:S(2)}) collective-permute-start(bf16[2,128,3584]{2,1,0:T(8,128)(2,1)S(1)} %pad_maximum_fusion.refs_0_.refs_6_), channel_id=1, source_target_pairs={{0,8},{8,0},{16,24},{24,16},{1,9},{9,1},{17,25},{25,17},{2,10},{10... | collective-permute-start | bytes 5505032 | tf_op jit(solution)/shard_map/ppermute | solution.py:451
  12.9 88.1 %collective-permute-start.2 = (bf16[2,128,3584]{2,1,0:T(8,128)(2,1)S(1)}, bf16[2,128,3584]{2,1,0:T(8,128)(2,1)}, u32[]{:S(2)}, u32[]{:S(2)}) collective-permute-start(bf16[2,128,3584]{2,1,0:T(8,128)(2,1)S(1)} %pad_maximum_fusion.refs_0_.refs_6_), channel_id=1, source_target_pairs={{0,24},{8,16},{16,8},{24,0},{1,25},{9,17},{17,9},{25,1},{2,26},{10... | collective-permute-start | bytes 5505032 | tf_op jit(solution)/shard_map/ppermute | solution.py:454
  16.6 83.5 %all-to-all-start = ((bf16[4,8,3584]{2,1,0:T(8,128)(2,1)}), bf16[4,8,3584]{2,1,0:T(8,128)(2,1)S(1)}, u32[]{:S(2)}, u32[]{:S(2)}) async-start(bf16[4,8,3584]{2,1,0:T(8,128)(2,1)} %bitcast.2), calls=%async_computation | async-start | bytes 458752 | tf_op jit(solution)/shard_map/all_to_all | solution.py:470
  20.0 108.3 %all-gather.6.cloned.1.call-start = ((), (), s32[]{:S(2)}) async-start(), calls=%async_computation.5 | async-start | bytes 2064384 | tf_op jit(solution)/shard_map/all_gather | solution.py:485
  62.9 38.1 %collective-permute-start = (bf16[3,304,128]{2,1,0:T(8,128)(2,1)}, bf16[3,304,128]{2,1,0:T(8,128)(2,1)S(1)}, u32[]{:S(2)}, u32[]{:S(2)}) collective-permute-start(bf16[3,304,128]{2,1,0:T(8,128)(2,1)} %get-tuple-element.76), channel_id=1, source_target_pairs={{0,1},{1,0},{2,3},{3,2},{4,5},{5,4},{6,7},{7,6},{8,9},{9,8},{10,11... | collective-permute-start | bytes 700424 | tf_op jit(solution)/shard_map/ppermute | solution.py:457
  100.9 16.9 %copy-start.11 = (bf16[3,304,128]{2,1,0:T(8,128)(2,1)}, bf16[3,304,128]{2,1,0:T(8,128)(2,1)S(1)}, u32[]{:S(2)}) copy-start(bf16[3,304,128]{2,1,0:T(8,128)(2,1)S(1)} %collective-permute-done.refs_1_) | copy-start | bytes 700420
  101.0 128.0 %reduce-scatter.2.cloned.1.call-start = ((), (), s32[]{:S(2)}) async-start(), calls=%async_computation.4 | async-start | bytes 1032192 | tf_op jit(solution)/shard_map/reduce_scatter | solution.py:495
  101.2 18.7 %collective-permute-start.6 = (bf16[2,128,3584]{2,1,0:T(8,128)(2,1)}, bf16[2,128,3584]{2,1,0:T(8,128)(2,1)}, u32[]{:S(2)}, u32[]{:S(2)}) collective-permute-start(bf16[2,128,3584]{2,1,0:T(8,128)(2,1)} %collective-permute-done.3.refs_0_.refs_8_), channel_id=1, source_target_pairs={{0,1},{1,0},{2,3},{3,2},{4,5},{5,4},{6,7},{7,6},{8,9},{9,8},{10,11... | collective-permute-start | bytes 5505032 | tf_op jit(solution)/shard_map/ppermute | solution.py:457
  101.3 18.7 %collective-permute-start.7 = (bf16[2,128,3584]{2,1,0:T(8,128)(2,1)}, bf16[2,128,3584]{2,1,0:T(8,128)(2,1)}, u32[]{:S(2)}, u32[]{:S(2)}) collective-permute-start(bf16[2,128,3584]{2,1,0:T(8,128)(2,1)} %collective-permute-done.2.refs_1_.refs_9_), channel_id=1, source_target_pairs={{0,1},{1,0},{2,3},{3,2},{4,5},{5,4},{6,7},{7,6},{8,9},{9,8},{10,11... | collective-permute-start | bytes 5505032 | tf_op jit(solution)/shard_map/ppermute | solution.py:457
  101.8 51.1 %collective-permute-start.4 = (bf16[2,128,3584]{2,1,0:T(8,128)(2,1)}, bf16[2,128,3584]{2,1,0:T(8,128)(2,1)S(1)}, u32[]{:S(2)}, u32[]{:S(2)}) collective-permute-start(bf16[2,128,3584]{2,1,0:T(8,128)(2,1)} %collective-permute-done.2.refs_1_.refs_9_), channel_id=1, source_target_pairs={{0,8},{8,0},{16,24},{24,16},{1,9},{9,1},{17,25},{25,17},{2,10},{10... | collective-permute-start | bytes 5505032 | tf_op jit(solution)/shard_map/ppermute | solution.py:451
  117.9 2.1 collective-permute-start.5
  120.0 33.0 %copy-start.10 = (bf16[3,304,256]{2,1,0:T(8,128)(2,1)}, bf16[3,304,256]{2,1,0:T(8,128)(2,1)S(1)}, u32[]{:S(2)}) copy-start(bf16[3,304,256]{2,1,0:T(8,128)(2,1)S(1)} %collective-permute-done.5.refs_3_) | copy-start | bytes 1400836
  152.9 1.2 copy-start.9
  153.0 16.3 %collective-permute-start.9 = (bf16[2,128,3584]{2,1,0:T(8,128)(2,1)S(1)}, bf16[2,128,3584]{2,1,0:T(8,128)(2,1)}, u32[]{:S(2)}, u32[]{:S(2)}) collective-permute-start(bf16[2,128,3584]{2,1,0:T(8,128)(2,1)S(1)} %collective-permute-done.4.refs_0_.refs_12_), channel_id=1, source_target_pairs={{0,1},{1,0},{2,3},{3,2},{4,5},{5,4},{6,7},{7,6},{8,9},{9,8},{10,11... | collective-permute-start | bytes 5505032 | tf_op jit(solution)/shard_map/ppermute | solution.py:457
  166.0 22.8 %collective-permute-start.10 = (bf16[128,3584]{1,0:T(8,128)(2,1)}, bf16[128,3584]{1,0:T(8,128)(2,1)S(1)}, u32[]{:S(2)}, u32[]{:S(2)}) collective-permute-start(bf16[128,3584]{1,0:T(8,128)(2,1)} %get-tuple-element.111), channel_id=1, source_target_pairs={{0,8},{8,0},{16,24},{24,16},{1,9},{9,1},{17,25},{25,17},{2,10},{10... | collective-permute-start | bytes 2752520 | tf_op jit(solution)/shard_map/ppermute | solution.py:451
  167.6 1.7 collective-permute-start.8
  169.3 0.7 copy-start.12
  177.5 14.3 %copy-start.15 = (bf16[128,3584]{1,0:T(8,128)(2,1)S(1)}, bf16[128,3584]{1,0:T(8,128)(2,1)}, u32[]{:S(2)}) copy-start(bf16[128,3584]{1,0:T(8,128)(2,1)} %get-tuple-element.124) | copy-start | bytes 2752516
  177.5 51.5 %collective-permute-start.12 = (bf16[3,160,1792]{2,1,0:T(8,128)(2,1)}, bf16[3,160,1792]{2,1,0:T(8,128)(2,1)}, u32[]{:S(2)}, u32[]{:S(2)}) collective-permute-start(bf16[3,160,1792]{2,1,0:T(8,128)(2,1)} %weight_terms.7), channel_id=1, source_target_pairs={{0,2},{1,3},{2,0},{3,1},{4,6},{5,7},{6,4},{7,5},{8,10},{9,11},{10,... | collective-permute-start | bytes 5160968 | tf_op jit(solution)/shard_map/ppermute | solution.py:457
  188.8 40.2 %collective-permute-start.13 = (bf16[3,144,1792]{2,1,0:T(8,128)(2,1)}, bf16[3,144,1792]{2,1,0:T(8,128)(2,1)}, u32[]{:S(2)}, u32[]{:S(2)}) collective-permute-start(bf16[3,144,1792]{2,1,0:T(8,128)(2,1)} %weight_terms.4), channel_id=1, source_target_pairs={{0,4},{1,5},{2,6},{3,7},{4,0},{5,1},{6,2},{7,3},{8,12},{9,13},{10,... | collective-permute-start | bytes 4644872 | tf_op jit(solution)/shard_map/ppermute | solution.py:457
  190.3 22.7 %collective-permute-start.11 = (bf16[128,3584]{1,0:T(8,128)(2,1)}, bf16[128,3584]{1,0:T(8,128)(2,1)}, u32[]{:S(2)}, u32[]{:S(2)}) collective-permute-start(bf16[128,3584]{1,0:T(8,128)(2,1)} %get-tuple-element.114), channel_id=1, source_target_pairs={{0,8},{8,0},{16,24},{24,16},{1,9},{9,1},{17,25},{25,17},{2,10},{10... | collective-permute-start | bytes 2752520 | tf_op jit(solution)/shard_map/ppermute | solution.py:451
  192.9 41.2 %collective-permute-start.16 = (bf16[128,3584]{1,0:T(8,128)(2,1)}, bf16[128,3584]{1,0:T(8,128)(2,1)}, u32[]{:S(2)}, u32[]{:S(2)}) collective-permute-start(bf16[128,3584]{1,0:T(8,128)(2,1)} %add_convert_fusion.1), channel_id=1, source_target_pairs={{0,24},{8,16},{16,8},{24,0},{1,25},{9,17},{17,9},{25,1},{2,26},{10... | collective-permute-start | bytes 2752520 | tf_op jit(solution)/shard_map/ppermute | solution.py:454
  202.5 29.2 %copy-start.1 = (bf16[3,144,1792]{2,1,0:T(8,128)(2,1)S(1)}, bf16[3,144,1792]{2,1,0:T(8,128)(2,1)}, u32[]{:S(2)}) copy-start(bf16[3,144,1792]{2,1,0:T(8,128)(2,1)} %weight_terms.6.refs_3_) | copy-start | bytes 4644868
  209.9 41.9 %copy-start = (bf16[3,160,1792]{2,1,0:T(8,128)(2,1)S(1)}, bf16[3,160,1792]{2,1,0:T(8,128)(2,1)}, u32[]{:S(2)}) copy-start(bf16[3,160,1792]{2,1,0:T(8,128)(2,1)} %weight_terms.5.refs_0_) | copy-start | bytes 5160964
  230.6 21.1 %collective-permute-start.14 = (bf16[3,160,896]{2,1,0:T(8,128)(2,1)S(1)}, bf16[3,160,896]{2,1,0:T(8,128)(2,1)S(1)}, u32[]{:S(2)}, u32[]{:S(2)}) collective-permute-start(bf16[3,160,896]{2,1,0:T(8,128)(2,1)S(1)} %add_convert_fusion.2), channel_id=1, source_target_pairs={{0,4},{1,5},{2,6},{3,7},{4,0},{5,1},{6,2},{7,3},{8,12},{9,13},{10,... | collective-permute-start | bytes 2580488 | tf_op jit(solution)/shard_map/ppermute | solution.py:457
  233.0 23.6 %copy-start.16 = (bf16[16,3584]{1,0:T(8,128)(2,1)S(1)}, bf16[16,3584]{1,0:T(8,128)(2,1)}, u32[]{:S(2)}) copy-start(bf16[16,3584]{1,0:T(8,128)(2,1)} %reduce-scatter.2.cloned.1.call-done) | copy-start | bytes 344068
  233.0 18.6 %collective-permute-start.15 = (bf16[3,144,896]{2,1,0:T(8,128)(2,1)S(1)}, bf16[3,144,896]{2,1,0:T(8,128)(2,1)S(1)}, u32[]{:S(2)}, u32[]{:S(2)}) collective-permute-start(bf16[3,144,896]{2,1,0:T(8,128)(2,1)S(1)} %add_convert_fusion.3), channel_id=1, source_target_pairs={{0,2},{1,3},{2,0},{3,1},{4,6},{5,7},{6,4},{7,5},{8,10},{9,11},{10,... | collective-permute-start | bytes 2322440 | tf_op jit(solution)/shard_map/ppermute | solution.py:457
  254.7 0.9 copy-start.4
  255.7 0.9 copy-start.7
  256.6 11.7 %copy-start.14 = (bf16[128,3584]{1,0:T(8,128)(2,1)S(1)}, bf16[128,3584]{1,0:T(8,128)(2,1)}, u32[]{:S(2)}) copy-start(bf16[128,3584]{1,0:T(8,128)(2,1)} %get-tuple-element.77) | copy-start | bytes 2752516
  257.3 10.5 %all-to-all-start.1 = ((bf16[4,4,3584]{2,1,0:T(4,128)(2,1)}), bf16[4,4,3584]{2,1,0:T(4,128)(2,1)S(1)}, u32[]{:S(2)}, u32[]{:S(2)}) async-start(bf16[4,4,3584]{2,1,0:T(4,128)(2,1)} %reshape.108), calls=%async_computation.2 | async-start | bytes 229376 | tf_op jit(solution)/shard_map/all_to_all | solution.py:78
  261.9 9.2 %collective-permute-start.17 = (bf16[3,304,448]{2,1,0:T(8,128)(2,1)}, bf16[3,304,448]{2,1,0:T(8,128)(2,1)S(1)}, u32[]{:S(2)}, u32[]{:S(2)}) collective-permute-start(bf16[3,304,448]{2,1,0:T(8,128)(2,1)} %copy-done.7), channel_id=1, source_target_pairs={{0,1},{1,0},{2,3},{3,2},{4,5},{5,4},{6,7},{7,6},{8,9},{9,8},{10,11... | collective-permute-start | bytes 2451464 | tf_op jit(solution)/shard_map/ppermute | solution.py:457
  271.1 0.9 copy-start.13
Sparse Core Ops, SparseCore 0:
  9.9 41.0 all-gather.3
  101.1 27.0 all-gather.5
  190.4 38.5 reduce-scatter.1

commit v3 on v2

--- a/solution.py
+++ b/solution.py
@@ -504,9 +504,9 @@
     low_kept = weight_terms(chip_tiles[2], acts, tokens, width, 0, cut)
     high_kept = weight_terms(chip_tiles[3], acts, tokens, width, cut, half)
     low_near, high_near = across(low_sent, 2), across(high_sent, 4)
+    from_mirror = mirror(add(mirrored_partial, from_last))
+    paired_partial, routed = together(paired_partial, routed)
     from_pair = pairs(paired_partial)
-    low_kept, high_kept, from_pair, routed = together(low_kept, high_kept, from_pair, routed)
-    from_mirror = mirror(add(mirrored_partial, from_last))
     low_near, high_near, low_kept, high_kept = together(
         low_near, high_near, low_kept, high_kept
     )
@@ -516,7 +516,7 @@
     mine, other = final_sum(
         core, (low_kept, low_near, low_far), (high_kept, high_near, high_far)
     )
-    mine, routed = together(mine, routed)
+    mine, routed, from_pair = together(mine, routed, from_pair)
     routed_input = to_tokens(slots_back(routed, experts), dispatch, me, experts)
     grads = join_halves(core, mine, across(other, 1))
     grad_input = (

time: 282 us -> 276 us (0.979)
  waiting for transfers between devices: 120 us -> 115 us
    reduce_scatter x1, waiting for transfers between devices: 16.1 us -> 0.01 us  [line_body(): routed = lax.psum_scatter(slot_terms, 'ep', scatter_dimension=0, tiled=True)]
    ppermute x12, waiting for transfers between devices: 21.3 us -> 30.6 us  [across(): return lax.ppermute(value, 'ep', [(i, i ^ apart) for i in range(8)])]
    ppermute x2, waiting for transfers between devices: 0.01 us -> 4.82 us  [mirror(): return lax.ppermute(value, 'tp', [(0, 3), (1, 2), (2, 1), (3, 0)])]
    ppermute x4, waiting for transfers between devices: 5.84 us -> 2.84 us  [pairs(): return lax.ppermute(value, 'tp', [(0, 1), (1, 0), (2, 3), (3, 2)])]
  transfers between devices with their start and end apart: 23 -> 23, of which waited for: 11 -> 10; matrix products, arithmetic and copies ran while one was open for 6% -> 6% of each run, Pallas kernels for 34% -> 35%
where the time goes in v3:
time: 276 us; the launch traced here: 275 us
  waiting for transfers between devices  115 us (42%)
  Pallas kernels  100 us (36%)
  starting transfers between devices  25.6 us (9%)
  between operations  14.1 us (5%)
  other arithmetic  12.1 us (4%)
  local copies, waits for them, and re-layouts  8.46 us (3%)
    pallas_call x3, Pallas kernels, dense_block(): pl.pallas_call(kernel, in_specs=[pl.BlockSpec(memory_space=pltpu.SMEM)] +...  39.8 us
    all_to_all x1, waiting for transfers between devices, line_body(): got = lax.all_to_all(sent, 'tp', split_axis=0, concat_axis=0, tiled=True)  35.4 us
    ppermute x12, waiting for transfers between devices, across(): return lax.ppermute(value, 'ep', [(i, i ^ apart) for i in range(8)])  30.6 us
    pallas_call x4, Pallas kernels, weight_terms(): pl.pallas_call(kernel, grid_spec=pltpu.PrefetchScalarGridSpec(num_scalar_...  29 us
    all_gather x1, waiting for transfers between devices, line_body(): down = lax.all_gather(dense_down.T, 'ep', axis=0, tiled=True)  26.3 us
    pallas_call x1, Pallas kernels, expert_block(): pl.pallas_call(kernel, in_specs=[vmem, hbm, hbm, hbm], out_specs=[hbm, hb...  24.7 us
    all_gather x1, waiting for transfers between devices, line_body(): slots = lax.all_gather(got, 'ep', axis=0, tiled=False)  8.27 us
    ppermute x12, starting transfers between devices, across(): return lax.ppermute(value, 'ep', [(i, i ^ apart) for i in range(8)])  6.89 us
  transfers between devices with their start and end apart: 23, of which 10 were waited for; matrix products, arithmetic and copies ran while one was open for 6% of the time, Pallas kernels for 35%

profile of v3, /device:TPU:0, one launch (start us, length us, event | category | flops | bytes accessed | tf_op | source)
XLA Modules:
  0.0 275.4 jit_solution(4149437278963467953)
XLA Ops:
  7.2 0.7 all-gather.4.cloned.1.call-update
  7.9 1.8 pad_maximum_fusion.refs_0_.refs_6_
  9.7 0.5 collective-permute-start.1
  10.2 2.7 collective-permute-start.3
  12.9 2.5 collective-permute-start.2
  15.4 1.2 routed_rows.1
  16.6 3.4 %all-to-all-start = ((bf16[4,8,3584]{2,1,0:T(8,128)(2,1)}), bf16[4,8,3584]{2,1,0:T(8,128)(2,1)S(1)}, u32[]{:S(2)}, u32[]{:S(2)}) async-start(bf16[4,8,3584]{2,1,0:T(8,128)(2,1)} %bitcast.2), calls=%async_computation | async-start | bytes 458752 | tf_op jit(solution)/shard_map/all_to_all | solution.py:470
  20.1 0.1 eq.56
  20.3 0.1 eq.52
  20.6 1.2 reduce-window.6
  22.2 0.1 copy.35
  22.5 0.1 copy.34
  22.6 0.3 eq.60
  23.0 0.3 eq.61
  23.3 0.3 mul.10
  23.7 0.3 mul.11
  24.0 0.7 pad_add_fusion
  24.7 26.3 %all-gather.4.cloned.1.call-done.refs_3_.refs_4_ = bf16[3584,608]{1,0:T(8,128)(2,1)} async-done(((bf16[448,608]{1,0:T(8,128)(2,1)}), bf16[3584,608]{1,0:T(8,128)(2,1)}) %all-gather.4.cloned.1.call-update) | async-done | bytes 4358160 | tf_op jit(solution)/shard_map/all_gather | solution.py:448
  51.0 11.8 %dense_block.3 = (bf16[3,304,128]{2,1,0:T(8,128)(2,1)}, bf16[3,304,128]{2,1,0:T(8,128)(2,1)}, bf16[128,3584]{1,0:T(8,128)(2,1)}) custom-call(s32[1]{0:T(128)} %bitcast.4.core_ref, bf16[2,128,3584]{2,1,0:T(8,128)(2,1)} %copy-done.8, bf16[608,3584]{1,0:T(8,128)(2,1)} %refs_1_.3, bf16[608,3584]{1,0:T(8,128)(2,1)} %refs_2_.5, ...), custom_call_target="tpu_custom_call" | custom-call | flops 2789212160 | bytes 16293888 | tf_op jit(solution)/shard_map/dense_block/pallas_call | solution.py:183
  62.8 0.3 collective-permute-start
  63.2 0.7 pad_add_fusion.2
  63.8 0.8 fusion.1
  64.7 35.4 %all-to-all-done = bf16[4,8,3584]{2,1,0:T(8,128)(2,1)S(1)} async-done(((bf16[4,8,3584]{2,1,0:T(8,128)(2,1)}), bf16[4,8,3584]{2,1,0:T(8,128)(2,1)S(1)}, u32[]{:S(2)}, u32[]{:S(2)}) %all-to-all-start) | async-done | bytes 229408 | tf_op jit(solution)/shard_map/all_to_all | solution.py:470
  100.2 0.7 reshape.104
  101.0 0.2 reduce-scatter.2.cloned.1.call-start
  101.3 0.5 collective-permute-start.7
  101.8 16.0 %dense_block.4 = (bf16[3,304,256]{2,1,0:T(8,128)(2,1)}, bf16[3,304,256]{2,1,0:T(8,128)(2,1)}, bf16[128,3584]{1,0:T(8,128)(2,1)}, bf16[128,3584]{1,0:T(8,128)(2,1)}) custom-call(s32[1]{0:T(128)} %bitcast.4.core_ref, bf16[2,128,3584]{2,1,0:T(8,128)(2,1)} %collective-permute-done.3.refs_0_.refs_8_, ...), custom_call_target="tpu_custom_call" | custom-call | flops 5578424320 | bytes 19513344 | tf_op jit(solution)/shard_map/dense_block/pallas_call | solution.py:183
  117.9 0.2 collective-permute-start.5
  118.0 1.9 collective-permute-done.5.refs_3_
  120.0 8.3 %all-gather.6.cloned.1.call-done = bf16[16,16,3584]{2,1,0:T(8,128)(2,1)} async-done(((bf16[2,16,3584]{2,1,0:T(8,128)(2,1)}), bf16[16,16,3584]{2,1,0:T(8,128)(2,1)}) %all-gather.6.cloned.1.call-update) | async-done | bytes 1835024 | tf_op jit(solution)/shard_map/all_gather | solution.py:485
  128.2 24.7 %expert_block.1 = (bf16[608,3584]{1,0:T(8,128)(2,1)}, bf16[608,3584]{1,0:T(8,128)(2,1)}, bf16[608,3584]{1,0:T(8,128)(2,1)}, bf16[128,3584]{1,0:T(8,128)(2,1)}) custom-call(bf16[8,2,16,3584]{3,2,1,0:T(8,128)(2,1)} %bitcast.49, bf16[608,3584]{1,0:T(8,128)(2,1)} %bitcast.46, bf16[608,3584]{1,0:T(8,128)(2,1)} %bitcast.47, bf16[608,3584]{1,0:T(8,128)(2,1)} %bitcast.48), custom_call_target="tpu_custom_call" | custom-call | flops 1 | bytes 1 | tf_op jit(solution)/shard_map/expert_block/pallas_call | solution.py:266
  153.0 0.3 collective-permute-start.9
  153.3 0.9 copy-done.9
  154.2 12.0 %dense_block.5 = (bf16[3,304,128]{2,1,0:T(8,128)(2,1)}, bf16[3,304,128]{2,1,0:T(8,128)(2,1)}, bf16[128,3584]{1,0:T(8,128)(2,1)}) custom-call(s32[1]{0:T(128)} %bitcast.4.core_ref, bf16[2,128,3584]{2,1,0:T(8,128)(2,1)} %copy-done.9, bf16[608,3584]{1,0:T(8,128)(2,1)} %refs_1_.3, bf16[608,3584]{1,0:T(8,128)(2,1)} %refs_2_.5, ...), custom_call_target="tpu_custom_call" | custom-call | flops 2789212160 | bytes 16293888 | tf_op jit(solution)/shard_map/dense_block/pallas_call | solution.py:183
  166.1 1.5 collective-permute-start.11
  167.7 1.7 collective-permute-done.8.refs_5_
  169.4 0.7 copy-done.12
  170.1 7.6 %weight_terms.4 = bf16[3,160,1792]{2,1,0:T(8,128)(2,1)} custom-call(s32[2]{0:T(128)} %get-tuple-element.77.tile_ref, bf16[3,304,128]{2,1,0:T(8,128)(2,1)} %get-tuple-element.78.refs_0_, bf16[3,304,128]{2,1,0:T(8,128)(2,1)} %copy-done.11, bf16[3,304,256]{2,1,0:T(8,128)(2,1)} %get-tuple-element.96.refs_2_, bf16[3,304,256]{2,1,0:T(8,128)(2,1)} %copy-done.10, ...), custom_call_target="tpu_custom_call" | custom-call | flops 1761607680 | bytes 10928128 | tf_op jit(solution)/shard_map/weight_terms/pallas_call | solution.py:364
  177.6 1.4 collective-permute-start.10
  179.1 7.0 %weight_terms.5 = bf16[3,144,1792]{2,1,0:T(8,128)(2,1)} custom-call(s32[2]{0:T(128)} %get-tuple-element.107.tile_ref, bf16[3,304,128]{2,1,0:T(8,128)(2,1)} %get-tuple-element.78.refs_0_, bf16[3,304,128]{2,1,0:T(8,128)(2,1)} %copy-done.11, bf16[3,304,256]{2,1,0:T(8,128)(2,1)} %get-tuple-element.96.refs_2_, bf16[3,304,256]{2,1,0:T(8,128)(2,1)} %copy-done.10, ...), custom_call_target="tpu_custom_call" | custom-call | flops 1585446912 | bytes 10756096 | tf_op jit(solution)/shard_map/weight_terms/pallas_call | solution.py:364
  186.1 2.8 %collective-permute-done.11 = bf16[128,3584]{1,0:T(8,128)(2,1)S(1)} collective-permute-done((bf16[128,3584]{1,0:T(8,128)(2,1)}, bf16[128,3584]{1,0:T(8,128)(2,1)S(1)}, u32[]{:S(2)}, u32[]{:S(2)}) %collective-permute-start.11) | collective-permute-done | bytes 917536 | tf_op jit(solution)/shard_map/ppermute | solution.py:451
  189.0 1.4 collective-permute-start.12
  190.3 1.5 collective-permute-start.16
  191.8 1.1 add_convert_fusion.1
  192.9 2.4 collective-permute-start.15
  195.3 7.0 %weight_terms.7.refs_3_ = bf16[3,144,1792]{2,1,0:T(8,128)(2,1)} custom-call(s32[2]{0:T(128)} %get-tuple-element.113.tile_ref, bf16[3,304,128]{2,1,0:T(8,128)(2,1)} %get-tuple-element.78.refs_0_, bf16[3,304,128]{2,1,0:T(8,128)(2,1)} %copy-done.11, bf16[3,304,256]{2,1,0:T(8,128)(2,1)} %get-tuple-element.96.refs_2_, bf16[3,304,256]{2,1,0:T(8,128)(2,1)} %copy-done.10, ...), custom_call_target="tpu_custom_call" | custom-call | flops 1585446912 | bytes 10756096 | tf_op jit(solution)/shard_map/weight_terms/pallas_call | solution.py:364
  202.3 7.4 %weight_terms.6.refs_0_ = bf16[3,160,1792]{2,1,0:T(8,128)(2,1)} custom-call(s32[2]{0:T(128)} %get-tuple-element.112.tile_ref, bf16[3,304,128]{2,1,0:T(8,128)(2,1)} %get-tuple-element.78.refs_0_, bf16[3,304,128]{2,1,0:T(8,128)(2,1)} %copy-done.11, bf16[3,304,256]{2,1,0:T(8,128)(2,1)} %get-tuple-element.96.refs_2_, bf16[3,304,256]{2,1,0:T(8,128)(2,1)} %copy-done.10, ...), custom_call_target="tpu_custom_call" | custom-call | flops 1761607680 | bytes 10928128 | tf_op jit(solution)/shard_map/weight_terms/pallas_call | solution.py:364
  209.7 14.9 %collective-permute-done.12.refs_4_ = bf16[3,144,1792]{2,1,0:T(8,128)(2,1)} collective-permute-done((bf16[3,144,1792]{2,1,0:T(8,128)(2,1)}, bf16[3,144,1792]{2,1,0:T(8,128)(2,1)}, u32[]{:S(2)}, u32[]{:S(2)}) %collective-permute-start.12) | collective-permute-done | bytes 1548320 | tf_op jit(solution)/shard_map/ppermute | solution.py:457
  224.6 1.4 add_convert_fusion.2
  226.0 1.4 collective-permute-start.13
  227.4 1.3 add_convert_fusion.3
  228.7 0.8 collective-permute-start.14
  229.5 4.8 %collective-permute-done.15 = bf16[128,3584]{1,0:T(8,128)(2,1)} collective-permute-done((bf16[128,3584]{1,0:T(8,128)(2,1)}, bf16[128,3584]{1,0:T(8,128)(2,1)}, u32[]{:S(2)}, u32[]{:S(2)}) %collective-permute-start.15) | collective-permute-done | bytes 917536 | tf_op jit(solution)/shard_map/ppermute | solution.py:454
  234.3 12.0 %collective-permute-done.14.refs_5_ = bf16[3,144,896]{2,1,0:T(8,128)(2,1)S(1)} collective-permute-done((bf16[3,144,896]{2,1,0:T(8,128)(2,1)S(1)}, bf16[3,144,896]{2,1,0:T(8,128)(2,1)S(1)}, u32[]{:S(2)}, u32[]{:S(2)}) %collective-permute-start.14) | collective-permute-done | bytes 774176 | tf_op jit(solution)/shard_map/ppermute | solution.py:457
  246.3 2.4 final_sum.1
  248.7 0.9 copy-done.4
  249.7 0.9 copy-done.7
  250.6 0.7 reshape.108
  251.3 4.6 %all-to-all-start.1 = ((bf16[4,4,3584]{2,1,0:T(4,128)(2,1)}), bf16[4,4,3584]{2,1,0:T(4,128)(2,1)S(1)}, u32[]{:S(2)}, u32[]{:S(2)}) async-start(bf16[4,4,3584]{2,1,0:T(4,128)(2,1)} %reshape.108), calls=%async_computation.2 | async-start | bytes 229376 | tf_op jit(solution)/shard_map/all_to_all | solution.py:78
  255.9 5.8 %all-to-all-done.1 = bf16[4,4,3584]{2,1,0:T(4,128)(2,1)S(1)} async-done(((bf16[4,4,3584]{2,1,0:T(4,128)(2,1)}), bf16[4,4,3584]{2,1,0:T(4,128)(2,1)S(1)}, u32[]{:S(2)}, u32[]{:S(2)}) %all-to-all-start.1) | async-done | bytes 114720 | tf_op jit(solution)/shard_map/all_to_all | solution.py:78
  261.7 0.5 convolution_bitcast_fusion
  262.2 2.8 %add_convert_fusion = bf16[128,3584]{1,0:T(8,128)(2,1)} fusion(f32[128,3584]{1,0:T(8,128)S(1)} %convolution_bitcast_fusion, bf16[128,3584]{1,0:T(8,128)(2,1)} %collective-permute-done.15, bf16[128,3584]{1,0:T(8,128)(2,1)} %collective-permute-done.16, bf16[128,3584]{1,0:T(8,128)(2,1)S(1)} %copy-done.14), kind=kLoop, calls=%fused_computation.2 | loop fusion | flops 3211264 | bytes 5505024 | tf_op jit(solution)/shard_map/convert_element_type | solution.py:527
  265.1 0.9 copy-done.13
  266.0 2.9 %join_halves.1 = (bf16[448,608]{1,0:T(8,128)(2,1)}, bf16[448,608]{1,0:T(8,128)(2,1)}, bf16[448,608]{1,0:T(8,128)(2,1)}) custom-call(s32[1]{0:T(128)} %bitcast.4.core_ref, bf16[3,304,448]{2,1,0:T(8,128)(2,1)} %copy-done.4, bf16[3,304,448]{2,1,0:T(8,128)(2,1)} %copy-done.13), custom_call_target="tpu_custom_call" | custom-call | bytes 3268608 | tf_op jit(solution)/shard_map/join_halves/pallas_call | solution.py:329
  (68 shorter events, 1.3 us)
Async XLA Ops:
  7.2 43.8 %all-gather.4.cloned.1.call-start = ((), (), s32[]{:S(2)}) async-start(), calls=%async_computation.3 | async-start | bytes 5160960 | tf_op jit(solution)/shard_map/all_gather | solution.py:448
  7.9 7.5 %copy-start.2 = (bf16[128,3584]{1,0:T(8,128)(2,1)S(1)}, bf16[128,3584]{1,0:T(8,128)(2,1)}, u32[]{:S(2)}) copy-start(bf16[128,3584]{1,0:T(8,128)(2,1)} %rows.1) | copy-start | bytes 2752516
  7.9 7.4 %copy-start.3 = (bf16[128,3584]{1,0:T(8,128)(2,1)S(1)}, bf16[128,3584]{1,0:T(8,128)(2,1)}, u32[]{:S(2)}) copy-start(bf16[128,3584]{1,0:T(8,128)(2,1)} %cots.1) | copy-start | bytes 2752516
  7.9 7.4 %copy-start.5 = (s32[128,2]{0,1:T(2,128)S(1)}, s32[128,2]{0,1:T(2,128)}, u32[]{:S(2)}) copy-start(s32[128,2]{0,1:T(2,128)} %param.12) | copy-start | bytes 3076
  7.9 7.4 %copy-start.6 = (f32[128,2]{0,1:T(2,128)S(1)}, f32[128,2]{0,1:T(2,128)}, u32[]{:S(2)}) copy-start(f32[128,2]{0,1:T(2,128)} %param.13) | copy-start | bytes 3076
  9.7 13.3 %copy-start.8 = (bf16[2,128,3584]{2,1,0:T(8,128)(2,1)}, bf16[2,128,3584]{2,1,0:T(8,128)(2,1)S(1)}, u32[]{:S(2)}) copy-start(bf16[2,128,3584]{2,1,0:T(8,128)(2,1)S(1)} %pad_maximum_fusion.refs_0_.refs_6_) | copy-start | bytes 5505028
  9.7 91.2 %collective-permute-start.1 = (bf16[2,128,3584]{2,1,0:T(8,128)(2,1)S(1)}, bf16[2,128,3584]{2,1,0:T(8,128)(2,1)}, u32[]{:S(2)}, u32[]{:S(2)}) collective-permute-start(bf16[2,128,3584]{2,1,0:T(8,128)(2,1)S(1)} %pad_maximum_fusion.refs_0_.refs_6_), channel_id=1, source_target_pairs={{0,1},{1,0},{2,3},{3,2},{4,5},{5,4},{6,7},{7,6},{8,9},{9,8},{10,11... | collective-permute-start | bytes 5505032 | tf_op jit(solution)/shard_map/ppermute | solution.py:457
  10.2 90.7 %collective-permute-start.3 = (bf16[2,128,3584]{2,1,0:T(8,128)(2,1)S(1)}, bf16[2,128,3584]{2,1,0:T(8,128)(2,1)}, u32[]{:S(2)}, u32[]{:S(2)}) collective-permute-start(bf16[2,128,3584]{2,1,0:T(8,128)(2,1)S(1)} %pad_maximum_fusion.refs_0_.refs_6_), channel_id=1, source_target_pairs={{0,8},{8,0},{16,24},{24,16},{1,9},{9,1},{17,25},{25,17},{2,10},{10... | collective-permute-start | bytes 5505032 | tf_op jit(solution)/shard_map/ppermute | solution.py:451
  12.9 88.1 %collective-permute-start.2 = (bf16[2,128,3584]{2,1,0:T(8,128)(2,1)S(1)}, bf16[2,128,3584]{2,1,0:T(8,128)(2,1)}, u32[]{:S(2)}, u32[]{:S(2)}) collective-permute-start(bf16[2,128,3584]{2,1,0:T(8,128)(2,1)S(1)} %pad_maximum_fusion.refs_0_.refs_6_), channel_id=1, source_target_pairs={{0,24},{8,16},{16,8},{24,0},{1,25},{9,17},{17,9},{25,1},{2,26},{10... | collective-permute-start | bytes 5505032 | tf_op jit(solution)/shard_map/ppermute | solution.py:454
  16.6 83.5 %all-to-all-start = ((bf16[4,8,3584]{2,1,0:T(8,128)(2,1)}), bf16[4,8,3584]{2,1,0:T(8,128)(2,1)S(1)}, u32[]{:S(2)}, u32[]{:S(2)}) async-start(bf16[4,8,3584]{2,1,0:T(8,128)(2,1)} %bitcast.2), calls=%async_computation | async-start | bytes 458752 | tf_op jit(solution)/shard_map/all_to_all | solution.py:470
  20.0 108.3 %all-gather.6.cloned.1.call-start = ((), (), s32[]{:S(2)}) async-start(), calls=%async_computation.5 | async-start | bytes 2064384 | tf_op jit(solution)/shard_map/all_gather | solution.py:485
  62.8 38.1 %collective-permute-start = (bf16[3,304,128]{2,1,0:T(8,128)(2,1)}, bf16[3,304,128]{2,1,0:T(8,128)(2,1)S(1)}, u32[]{:S(2)}, u32[]{:S(2)}) collective-permute-start(bf16[3,304,128]{2,1,0:T(8,128)(2,1)} %get-tuple-element.75), channel_id=1, source_target_pairs={{0,1},{1,0},{2,3},{3,2},{4,5},{5,4},{6,7},{7,6},{8,9},{9,8},{10,11... | collective-permute-start | bytes 700424 | tf_op jit(solution)/shard_map/ppermute | solution.py:457
  100.9 16.9 %copy-start.11 = (bf16[3,304,128]{2,1,0:T(8,128)(2,1)}, bf16[3,304,128]{2,1,0:T(8,128)(2,1)S(1)}, u32[]{:S(2)}) copy-start(bf16[3,304,128]{2,1,0:T(8,128)(2,1)S(1)} %collective-permute-done.refs_1_) | copy-start | bytes 700420
  101.0 89.3 %reduce-scatter.2.cloned.1.call-start = ((), (), s32[]{:S(2)}) async-start(), calls=%async_computation.4 | async-start | bytes 1032192 | tf_op jit(solution)/shard_map/reduce_scatter | solution.py:495
  101.2 18.7 %collective-permute-start.6 = (bf16[2,128,3584]{2,1,0:T(8,128)(2,1)}, bf16[2,128,3584]{2,1,0:T(8,128)(2,1)}, u32[]{:S(2)}, u32[]{:S(2)}) collective-permute-start(bf16[2,128,3584]{2,1,0:T(8,128)(2,1)} %collective-permute-done.3.refs_0_.refs_8_), channel_id=1, source_target_pairs={{0,1},{1,0},{2,3},{3,2},{4,5},{5,4},{6,7},{7,6},{8,9},{9,8},{10,11... | collective-permute-start | bytes 5505032 | tf_op jit(solution)/shard_map/ppermute | solution.py:457
  101.3 18.7 %collective-permute-start.7 = (bf16[2,128,3584]{2,1,0:T(8,128)(2,1)}, bf16[2,128,3584]{2,1,0:T(8,128)(2,1)}, u32[]{:S(2)}, u32[]{:S(2)}) collective-permute-start(bf16[2,128,3584]{2,1,0:T(8,128)(2,1)} %collective-permute-done.2.refs_1_.refs_9_), channel_id=1, source_target_pairs={{0,1},{1,0},{2,3},{3,2},{4,5},{5,4},{6,7},{7,6},{8,9},{9,8},{10,11... | collective-permute-start | bytes 5505032 | tf_op jit(solution)/shard_map/ppermute | solution.py:457
  101.8 51.1 %collective-permute-start.4 = (bf16[2,128,3584]{2,1,0:T(8,128)(2,1)}, bf16[2,128,3584]{2,1,0:T(8,128)(2,1)S(1)}, u32[]{:S(2)}, u32[]{:S(2)}) collective-permute-start(bf16[2,128,3584]{2,1,0:T(8,128)(2,1)} %collective-permute-done.2.refs_1_.refs_9_), channel_id=1, source_target_pairs={{0,8},{8,0},{16,24},{24,16},{1,9},{9,1},{17,25},{25,17},{2,10},{10... | collective-permute-start | bytes 5505032 | tf_op jit(solution)/shard_map/ppermute | solution.py:451
  117.9 2.1 collective-permute-start.5
  120.0 33.0 %copy-start.10 = (bf16[3,304,256]{2,1,0:T(8,128)(2,1)}, bf16[3,304,256]{2,1,0:T(8,128)(2,1)S(1)}, u32[]{:S(2)}) copy-start(bf16[3,304,256]{2,1,0:T(8,128)(2,1)S(1)} %collective-permute-done.5.refs_3_) | copy-start | bytes 1400836
  152.9 1.2 copy-start.9
  153.0 16.4 %collective-permute-start.9 = (bf16[2,128,3584]{2,1,0:T(8,128)(2,1)S(1)}, bf16[2,128,3584]{2,1,0:T(8,128)(2,1)}, u32[]{:S(2)}, u32[]{:S(2)}) collective-permute-start(bf16[2,128,3584]{2,1,0:T(8,128)(2,1)S(1)} %collective-permute-done.4.refs_0_.refs_12_), channel_id=1, source_target_pairs={{0,1},{1,0},{2,3},{3,2},{4,5},{5,4},{6,7},{7,6},{8,9},{9,8},{10,11... | collective-permute-start | bytes 5505032 | tf_op jit(solution)/shard_map/ppermute | solution.py:457
  166.1 22.8 %collective-permute-start.11 = (bf16[128,3584]{1,0:T(8,128)(2,1)}, bf16[128,3584]{1,0:T(8,128)(2,1)S(1)}, u32[]{:S(2)}, u32[]{:S(2)}) collective-permute-start(bf16[128,3584]{1,0:T(8,128)(2,1)} %get-tuple-element.110), channel_id=1, source_target_pairs={{0,8},{8,0},{16,24},{24,16},{1,9},{9,1},{17,25},{25,17},{2,10},{10... | collective-permute-start | bytes 2752520 | tf_op jit(solution)/shard_map/ppermute | solution.py:451
  167.7 1.7 collective-permute-start.8
  169.4 0.7 copy-start.12
  177.6 14.1 %copy-start.15 = (bf16[128,3584]{1,0:T(8,128)(2,1)S(1)}, bf16[128,3584]{1,0:T(8,128)(2,1)}, u32[]{:S(2)}) copy-start(bf16[128,3584]{1,0:T(8,128)(2,1)} %get-tuple-element.118) | copy-start | bytes 2752516
  177.6 47.0 %collective-permute-start.10 = (bf16[3,160,1792]{2,1,0:T(8,128)(2,1)}, bf16[3,160,1792]{2,1,0:T(8,128)(2,1)S(1)}, u32[]{:S(2)}, u32[]{:S(2)}) collective-permute-start(bf16[3,160,1792]{2,1,0:T(8,128)(2,1)} %weight_terms.4), channel_id=1, source_target_pairs={{0,2},{1,3},{2,0},{3,1},{4,6},{5,7},{6,4},{7,5},{8,10},{9,11},{10,... | collective-permute-start | bytes 5160968 | tf_op jit(solution)/shard_map/ppermute | solution.py:457
  189.0 35.7 %collective-permute-start.12 = (bf16[3,144,1792]{2,1,0:T(8,128)(2,1)}, bf16[3,144,1792]{2,1,0:T(8,128)(2,1)}, u32[]{:S(2)}, u32[]{:S(2)}) collective-permute-start(bf16[3,144,1792]{2,1,0:T(8,128)(2,1)} %weight_terms.5), channel_id=1, source_target_pairs={{0,4},{1,5},{2,6},{3,7},{4,0},{5,1},{6,2},{7,3},{8,12},{9,13},{10,... | collective-permute-start | bytes 4644872 | tf_op jit(solution)/shard_map/ppermute | solution.py:457
  190.3 60.3 %collective-permute-start.16 = (bf16[128,3584]{1,0:T(8,128)(2,1)}, bf16[128,3584]{1,0:T(8,128)(2,1)}, u32[]{:S(2)}, u32[]{:S(2)}) collective-permute-start(bf16[128,3584]{1,0:T(8,128)(2,1)} %get-tuple-element.126), channel_id=1, source_target_pairs={{0,8},{8,0},{16,24},{24,16},{1,9},{9,1},{17,25},{25,17},{2,10},{10... | collective-permute-start | bytes 2752520 | tf_op jit(solution)/shard_map/ppermute | solution.py:451
  192.9 41.4 %collective-permute-start.15 = (bf16[128,3584]{1,0:T(8,128)(2,1)}, bf16[128,3584]{1,0:T(8,128)(2,1)}, u32[]{:S(2)}, u32[]{:S(2)}) collective-permute-start(bf16[128,3584]{1,0:T(8,128)(2,1)} %add_convert_fusion.1), channel_id=1, source_target_pairs={{0,24},{8,16},{16,8},{24,0},{1,25},{9,17},{17,9},{25,1},{2,26},{10... | collective-permute-start | bytes 2752520 | tf_op jit(solution)/shard_map/ppermute | solution.py:454
  202.3 25.1 %copy-start.1 = (bf16[3,144,1792]{2,1,0:T(8,128)(2,1)S(1)}, bf16[3,144,1792]{2,1,0:T(8,128)(2,1)}, u32[]{:S(2)}) copy-start(bf16[3,144,1792]{2,1,0:T(8,128)(2,1)} %weight_terms.7.refs_3_) | copy-start | bytes 4644868
  209.7 36.6 %copy-start = (bf16[3,160,1792]{2,1,0:T(8,128)(2,1)S(1)}, bf16[3,160,1792]{2,1,0:T(8,128)(2,1)}, u32[]{:S(2)}) copy-start(bf16[3,160,1792]{2,1,0:T(8,128)(2,1)} %weight_terms.6.refs_0_) | copy-start | bytes 5160964
  226.0 20.3 %collective-permute-start.13 = (bf16[3,160,896]{2,1,0:T(8,128)(2,1)S(1)}, bf16[3,160,896]{2,1,0:T(8,128)(2,1)S(1)}, u32[]{:S(2)}, u32[]{:S(2)}) collective-permute-start(bf16[3,160,896]{2,1,0:T(8,128)(2,1)S(1)} %add_convert_fusion.2), channel_id=1, source_target_pairs={{0,4},{1,5},{2,6},{3,7},{4,0},{5,1},{6,2},{7,3},{8,12},{9,13},{10,... | collective-permute-start | bytes 2580488 | tf_op jit(solution)/shard_map/ppermute | solution.py:457
  228.7 21.9 %copy-start.17 = (bf16[16,3584]{1,0:T(8,128)(2,1)S(1)}, bf16[16,3584]{1,0:T(8,128)(2,1)}, u32[]{:S(2)}) copy-start(bf16[16,3584]{1,0:T(8,128)(2,1)} %reduce-scatter.2.cloned.1.call-done) | copy-start | bytes 344068
  228.7 27.2 %copy-start.16 = (bf16[128,16]{1,0:T(8,128)(2,1)S(1)}, bf16[128,16]{1,0:T(8,128)(2,1)}, u32[]{:S(2)}) copy-start(bf16[128,16]{1,0:T(8,128)(2,1)} %fusion.1) | copy-start | bytes 12292
  228.7 17.6 %collective-permute-start.14 = (bf16[3,144,896]{2,1,0:T(8,128)(2,1)S(1)}, bf16[3,144,896]{2,1,0:T(8,128)(2,1)S(1)}, u32[]{:S(2)}, u32[]{:S(2)}) collective-permute-start(bf16[3,144,896]{2,1,0:T(8,128)(2,1)S(1)} %add_convert_fusion.3), channel_id=1, source_target_pairs={{0,2},{1,3},{2,0},{3,1},{4,6},{5,7},{6,4},{7,5},{8,10},{9,11},{10,... | collective-permute-start | bytes 2322440 | tf_op jit(solution)/shard_map/ppermute | solution.py:457
  248.7 1.0 copy-start.4
  249.6 0.9 copy-start.7
  250.6 11.6 %copy-start.14 = (bf16[128,3584]{1,0:T(8,128)(2,1)S(1)}, bf16[128,3584]{1,0:T(8,128)(2,1)}, u32[]{:S(2)}) copy-start(bf16[128,3584]{1,0:T(8,128)(2,1)} %get-tuple-element.76) | copy-start | bytes 2752516
  251.3 10.4 %all-to-all-start.1 = ((bf16[4,4,3584]{2,1,0:T(4,128)(2,1)}), bf16[4,4,3584]{2,1,0:T(4,128)(2,1)S(1)}, u32[]{:S(2)}, u32[]{:S(2)}) async-start(bf16[4,4,3584]{2,1,0:T(4,128)(2,1)} %reshape.108), calls=%async_computation.2 | async-start | bytes 229376 | tf_op jit(solution)/shard_map/all_to_all | solution.py:78
  255.9 9.2 %collective-permute-start.17 = (bf16[3,304,448]{2,1,0:T(8,128)(2,1)}, bf16[3,304,448]{2,1,0:T(8,128)(2,1)S(1)}, u32[]{:S(2)}, u32[]{:S(2)}) collective-permute-start(bf16[3,304,448]{2,1,0:T(8,128)(2,1)} %copy-done.7), channel_id=1, source_target_pairs={{0,1},{1,0},{2,3},{3,2},{4,5},{5,4},{6,7},{7,6},{8,9},{9,8},{10,11... | collective-permute-start | bytes 2451464 | tf_op jit(solution)/shard_map/ppermute | solution.py:457
  265.1 0.9 copy-start.13
Sparse Core Ops, SparseCore 0:
  9.9 41.0 all-gather.3
  101.1 27.0 all-gather.5
  153.4 36.5 reduce-scatter.1
